TPU v7x, 512 devices: a whole 4x8x8 slice. The times are simulated.
512 devices in a mesh: lon: 32 (over x, y), lat: 16 (over z, core).
Axes of the slice: x: 4, y: 8, z: 8, core: 2. Of those that a mesh axis runs over, the one named last changes fastest.
Arguments:
- tracer: float32 [2, 25, 128, 4096], P(None, None, 'lat', 'lon'), may hold values from -6 to 6
- ocean_mask: int32 [25, 128, 4096], P(None, 'lat', 'lon'), may hold values from 0 to 1, as said below
- kappa_lon: bfloat16 [25, 128, 4096], P(None, 'lat', 'lon'), may hold values from 0.049804688 to 0.23925781
- kappa_lat: bfloat16 [25, 128, 4096], P(None, 'lat', 'lon'), may hold values from 4 to 256
- vertical_root: float32 [2, 25, 25], replicated, may hold values from -1.25 to 1.25
Outputs:
- correlated: float32 [2, 25, 128, 4096], P(None, None, 'lat', 'lon')
Inputs may be any that keep to these rules, and one draw needn't show every extreme that they name: `ocean_mask`: 0 or 1; a cell that is land at one level is land at every deeper level.
All inputs are finite; a program needn't handle non-finite values.
Results may differ from a plain program's by a relative error of at most 0.0003.
Values sent between devices are 32-bit elements; how exact they have to be, the bound alone decides.
A program may use at most 64 MiB of HBM per device.

v0:
```python
import jax
import jax.numpy as jnp
from jax import lax
from jax.sharding import PartitionSpec as P

STEPS = 4


def with_halo(cells, sides, width):
    for axis, dim in sides:
        count = lax.axis_size(axis)
        head = lax.slice_in_dim(cells, 0, width, axis=dim)
        tail = lax.slice_in_dim(cells, cells.shape[dim] - width, cells.shape[dim], axis=dim)
        cells = jnp.concatenate(
            [
                lax.ppermute(tail, axis, [(i, (i + 1) % count) for i in range(count)]),
                cells,
                lax.ppermute(head, axis, [((i + 1) % count, i) for i in range(count)]),
            ],
            axis=dim,
        )
    return cells


def lon_step(state, coefficient):
    face_east = jnp.minimum(coefficient[..., :-1], coefficient[..., 1:])
    east_flux = face_east * (state[..., 1:] - state[..., :-1])
    updated = state[..., 1:-1] + east_flux[..., 1:] - east_flux[..., :-1]
    return (updated, coefficient[..., 1:-1])


def face_inside(coefficient, along):
    count = coefficient.shape[along]
    rows_all = lax.broadcasted_iota(jnp.int32, coefficient.shape, along)
    upper_face = jnp.where(
        rows_all < count - 1, jnp.minimum(coefficient, jnp.roll(coefficient, -1, axis=along)), 0.0
    )
    lower_face = jnp.where(rows_all > 0, jnp.roll(upper_face, 1, axis=along), 0.0)
    return (lower_face, upper_face)


def compose_forward(former, latter):
    top_left = latter[0] * former[0] + latter[1] * former[2]
    top_right = latter[0] * former[1] + latter[1] * former[3]
    low_left = latter[2] * former[0] + latter[3] * former[2]
    low_right = latter[2] * former[1] + latter[3] * former[3]
    decay = latter[4] * former[4]
    first_term = latter[4] * former[5] + latter[5] * former[0] + latter[6] * former[2]
    second_term = latter[4] * former[6] + latter[5] * former[1] + latter[6] * former[3]
    inverse = 1.0 / low_right
    return (
        top_left * inverse,
        top_right * inverse,
        low_left * inverse,
        low_right * inverse,
        decay * inverse,
        first_term * inverse,
        second_term * inverse,
    )


def compose_backward(former, latter):
    return (latter[0] * former[0], latter[1] + latter[0] * former[1])


def forward_local(values, lower_face, upper_face, along):
    zero_face = jnp.zeros_like(upper_face)
    elements = (
        zero_face,
        upper_face,
        -lower_face,
        1.0 + lower_face + upper_face,
        lower_face,
        jnp.zeros_like(values),
        values,
    )
    return lax.associative_scan(compose_forward, elements, axis=along)


def to_backward(prefix):
    return (prefix[1] / prefix[3], prefix[6] / prefix[3])


def backward_local(affine, along):
    flipped = tuple((jnp.flip(leaf, axis=along) for leaf in affine))
    scanned = lax.associative_scan(compose_backward, flipped, axis=along)
    return tuple((jnp.flip(leaf, axis=along) for leaf in scanned))


def solve_columns(stacked):
    shape_in = stacked.shape
    leading = jnp.moveaxis(stacked, 2, 0)
    flat = leading.reshape(shape_in[2], shape_in[0], shape_in[1] * shape_in[3])
    values = flat[:, :2]
    lower_face, upper_face = face_inside(flat[:, 2:3], 0)
    prefix = forward_local(values, lower_face, upper_face, 0)
    local_maps = backward_local(to_backward(prefix), 0)
    solved_flat = local_maps[1].reshape(shape_in[2], 2, shape_in[1], shape_in[3])
    solved_cols = jnp.moveaxis(solved_flat, 0, 2)
    return lax.all_to_all(solved_cols, "lat", split_axis=2, concat_axis=3, tiled=True)


def per_device(tracer, ocean_mask, kappa_lon, kappa_lat, vertical_root):
    ocean = ocean_mask.astype(jnp.float32)[None]
    state = tracer * ocean
    coef_lon = kappa_lon.astype(jnp.float32)[None] * ocean
    coef_lat = kappa_lat.astype(jnp.float32)[None] * ocean
    coef_ext = with_halo(coef_lon, (("lon", 3),), 1)
    for sweep in range(STEPS):
        extended = with_halo(state, (("lon", 3),), 1)
        state, unused = lon_step(extended, coef_ext)
    stacked = jnp.concatenate([state, coef_lat], axis=0)
    solved = solve_columns(lax.all_to_all(stacked, "lat", split_axis=3, concat_axis=2, tiled=True))
    mixed = jnp.einsum("flk,fkyx->flyx", vertical_root, solved, precision=lax.Precision.HIGHEST)
    return mixed * ocean


def solution(mesh):
    placed = (
        P(None, None, "lat", "lon"),
        P(None, "lat", "lon"),
        P(None, "lat", "lon"),
        P(None, "lat", "lon"),
        P(),
    )
    return jax.shard_map(
        per_device,
        mesh=mesh,
        in_specs=placed,
        out_specs=P(None, None, "lat", "lon"),
        check_vma=False,
    )
```

profile of v0, /device:TPU:1, one launch (start us, length us, event | category | flops | bytes accessed | tf_op | source)
XLA Modules:
  0.0 309.1 jit_solution(1422311900136746580)
XLA Ops:
  1.1 4.0 %collective-permute-start = (f32[1,25,8,1]{3,2,1,0:T(8,128)S(1)}, f32[1,25,8,1]{3,2,1,0:T(8,128)S(1)}, u32[]{:S(2)}, u32[]{:S(2)}) collective-permute-start(f32[1,25,8,1]{3,2,1,0:T(8,128)S(1)} %get-tuple-element.118), channel_id=1, source_target_pairs={{0,16},{16,32},{32,48},{48,64},{64,80},{80,96},{96,112},{112,128},... | collective-permute-start | bytes 2408 | tf_op jit(solution)/shard_map/ppermute | solution.py:16
  5.1 6.0 %collective-permute-start.1 = (f32[1,25,8,1]{3,2,1,0:T(8,128)S(1)}, f32[1,25,8,1]{3,2,1,0:T(8,128)S(1)}, u32[]{:S(2)}, u32[]{:S(2)}) collective-permute-start(f32[1,25,8,1]{3,2,1,0:T(8,128)S(1)} %get-tuple-element.117), channel_id=1, source_target_pairs={{16,0},{32,16},{48,32},{64,48},{80,64},{96,80},{112,96},{128,112},... | collective-permute-start | bytes 2408 | tf_op jit(solution)/shard_map/ppermute | solution.py:18
  13.2 3.5 %collective-permute-start.2 = (f32[2,25,8,1]{3,1,2,0:T(8,128)S(1)}, f32[2,25,8,1]{3,1,2,0:T(8,128)S(1)}, u32[]{:S(2)}, u32[]{:S(2)}) collective-permute-start(f32[2,25,8,1]{3,1,2,0:T(8,128)S(1)} %get-tuple-element.44), channel_id=1, source_target_pairs={{16,0},{32,16},{48,32},{64,48},{80,64},{96,80},{112,96},{128,112},... | collective-permute-start | bytes 4808 | tf_op jit(solution)/shard_map/ppermute | solution.py:18
  16.7 1.9 collective-permute-start.3
  21.1 6.0 %collective-permute-done.3 = f32[2,25,8,1]{3,1,2,0:T(8,128)S(1)} collective-permute-done((f32[2,25,8,1]{3,1,2,0:T(8,128)S(1)}, f32[2,25,8,1]{3,1,2,0:T(8,128)S(1)}, u32[]{:S(2)}, u32[]{:S(2)}) %collective-permute-start.3) | collective-permute-done | bytes 1632 | tf_op jit(solution)/shard_map/ppermute | solution.py:16
  27.7 1.9 collective-permute-start.4
  29.6 3.4 %collective-permute-start.5 = (f32[2,25,8,1]{3,1,2,0:T(8,128)S(1)}, f32[2,25,8,1]{3,1,2,0:T(8,128)S(1)}, u32[]{:S(2)}, u32[]{:S(2)}) collective-permute-start(f32[2,25,8,1]{3,1,2,0:T(8,128)S(1)} %get-tuple-element.41), channel_id=1, source_target_pairs={{0,16},{16,32},{32,48},{48,64},{64,80},{80,96},{96,112},{112,128},... | collective-permute-start | bytes 4808 | tf_op jit(solution)/shard_map/ppermute | solution.py:16
  34.8 5.2 %collective-permute-done.5 = f32[2,25,8,1]{3,1,2,0:T(8,128)S(1)} collective-permute-done((f32[2,25,8,1]{3,1,2,0:T(8,128)S(1)}, f32[2,25,8,1]{3,1,2,0:T(8,128)S(1)}, u32[]{:S(2)}, u32[]{:S(2)}) %collective-permute-start.5) | collective-permute-done | bytes 1632 | tf_op jit(solution)/shard_map/ppermute | solution.py:16
  42.5 3.4 %collective-permute-start.7 = (f32[2,25,8,1]{3,1,2,0:T(8,128)S(1)}, f32[2,25,8,1]{3,1,2,0:T(8,128)S(1)}, u32[]{:S(2)}, u32[]{:S(2)}) collective-permute-start(f32[2,25,8,1]{3,1,2,0:T(8,128)S(1)} %get-tuple-element.39), channel_id=1, source_target_pairs={{0,16},{16,32},{32,48},{48,64},{64,80},{80,96},{96,112},{112,128},... | collective-permute-start | bytes 4808 | tf_op jit(solution)/shard_map/ppermute | solution.py:16
  47.7 5.2 %collective-permute-done.7 = f32[2,25,8,1]{3,1,2,0:T(8,128)S(1)} collective-permute-done((f32[2,25,8,1]{3,1,2,0:T(8,128)S(1)}, f32[2,25,8,1]{3,1,2,0:T(8,128)S(1)}, u32[]{:S(2)}, u32[]{:S(2)}) %collective-permute-start.7) | collective-permute-done | bytes 1632 | tf_op jit(solution)/shard_map/ppermute | solution.py:16
  55.3 3.4 %collective-permute-start.9 = (f32[2,25,8,1]{3,1,2,0:T(8,128)S(1)}, f32[2,25,8,1]{3,1,2,0:T(8,128)S(1)}, u32[]{:S(2)}, u32[]{:S(2)}) collective-permute-start(f32[2,25,8,1]{3,1,2,0:T(8,128)S(1)} %get-tuple-element.37), channel_id=1, source_target_pairs={{0,16},{16,32},{32,48},{48,64},{64,80},{80,96},{96,112},{112,128},... | collective-permute-start | bytes 4808 | tf_op jit(solution)/shard_map/ppermute | solution.py:16
  60.5 5.2 %collective-permute-done.9 = f32[2,25,8,1]{3,1,2,0:T(8,128)S(1)} collective-permute-done((f32[2,25,8,1]{3,1,2,0:T(8,128)S(1)}, f32[2,25,8,1]{3,1,2,0:T(8,128)S(1)}, u32[]{:S(2)}, u32[]{:S(2)}) %collective-permute-start.9) | collective-permute-done | bytes 1632 | tf_op jit(solution)/shard_map/ppermute | solution.py:16
  66.7 2.3 reshape.185
  69.0 17.4 %all-to-all-start = ((f32[16,1,4800]{2,1,0:T(1,128)}), f32[16,1,4800]{2,1,0:T(1,128)S(1)}, u32[]{:S(2)}, u32[]{:S(2)}) async-start(f32[16,1,4800]{2,1,0:T(1,128)} %reshape.185), calls=%async_computation | async-start | bytes 622592 | tf_op jit(solution)/shard_map/all_to_all | solution.py:113
  86.5 12.5 %all-to-all-done = f32[16,1,4800]{2,1,0:T(1,128)S(1)} async-done(((f32[16,1,4800]{2,1,0:T(1,128)}), f32[16,1,4800]{2,1,0:T(1,128)S(1)}, u32[]{:S(2)}, u32[]{:S(2)}) %all-to-all-start) | async-done | bytes 307232 | tf_op jit(solution)/shard_map/all_to_all | solution.py:113
  114.9 2.0 slice.836
  118.7 4.1 %slice.834 = f32[64,2,200]{0,2,1:T(8,128)} slice(f32[128,2,200]{0,2,1:T(8,128)S(1)} %slice.1077), slice={[1:128:2], [0:2:1], [0:200:1]} | slice | bytes 204800 | tf_op jit(solution)/shard_map/slice | solution.py:77
  122.8 4.0 %slice.832 = f32[64,2,200]{0,2,1:T(8,128)} slice(f32[128,2,200]{0,2,1:T(8,128)S(1)} %slice.1077), slice={[0:127:2], [0:2:1], [0:200:1]} | slice | bytes 204800 | tf_op jit(solution)/shard_map/slice | solution.py:77
  159.2 2.0 multiply_multiply_fusion
  176.2 2.0 fusion.105
  200.8 4.1 %slice.988 = f32[63,2,200]{0,2,1:T(8,128)} slice(f32[128,2,200]{0,2,1:T(8,128)S(1)} %slice.1077), slice={[2:128:2], [0:2:1], [0:200:1]} | slice | bytes 201600 | tf_op jit(solution)/shard_map/slice | solution.py:77
  208.4 2.1 slice.991
  210.6 2.4 slice.829
  291.5 13.2 %all_to_all.36 = f32[16,1,3200]{2,1,0:T(1,128)S(1)} all-to-all(f32[16,1,3200]{2,1,0:T(1,128)S(1)} %reshape.187), channel_id=1, replica_groups=mesh['lon'=32,'lat'=16] {'lat'}, dimensions={0} | all-to-all | bytes 409600 | tf_op jit(solution)/shard_map/all_to_all | solution.py:100
  (684 shorter events, 188.7 us)
Async XLA Ops:
  0.0 306.8 %copy-start = (f32[2,25,25]{2,0,1:T(2,128)S(1)}, f32[2,25,25]{2,0,1:T(2,128)}, u32[]{:S(2)}) copy-start(f32[2,25,25]{2,0,1:T(2,128)} %param.9) | copy-start | bytes 15004
  1.1 17.5 %collective-permute-start = (f32[1,25,8,1]{3,2,1,0:T(8,128)S(1)}, f32[1,25,8,1]{3,2,1,0:T(8,128)S(1)}, u32[]{:S(2)}, u32[]{:S(2)}) collective-permute-start(f32[1,25,8,1]{3,2,1,0:T(8,128)S(1)} %get-tuple-element.118), channel_id=1, source_target_pairs={{0,16},{16,32},{32,48},{48,64},{64,80},{80,96},{96,112},{112,128},... | collective-permute-start | bytes 2408 | tf_op jit(solution)/shard_map/ppermute | solution.py:16
  5.1 13.8 %collective-permute-start.1 = (f32[1,25,8,1]{3,2,1,0:T(8,128)S(1)}, f32[1,25,8,1]{3,2,1,0:T(8,128)S(1)}, u32[]{:S(2)}, u32[]{:S(2)}) collective-permute-start(f32[1,25,8,1]{3,2,1,0:T(8,128)S(1)} %get-tuple-element.117), channel_id=1, source_target_pairs={{16,0},{32,16},{48,32},{64,48},{80,64},{96,80},{112,96},{128,112},... | collective-permute-start | bytes 2408 | tf_op jit(solution)/shard_map/ppermute | solution.py:18
  13.2 7.9 %collective-permute-start.2 = (f32[2,25,8,1]{3,1,2,0:T(8,128)S(1)}, f32[2,25,8,1]{3,1,2,0:T(8,128)S(1)}, u32[]{:S(2)}, u32[]{:S(2)}) collective-permute-start(f32[2,25,8,1]{3,1,2,0:T(8,128)S(1)} %get-tuple-element.44), channel_id=1, source_target_pairs={{16,0},{32,16},{48,32},{64,48},{80,64},{96,80},{112,96},{128,112},... | collective-permute-start | bytes 4808 | tf_op jit(solution)/shard_map/ppermute | solution.py:18
  16.7 10.4 %collective-permute-start.3 = (f32[2,25,8,1]{3,1,2,0:T(8,128)S(1)}, f32[2,25,8,1]{3,1,2,0:T(8,128)S(1)}, u32[]{:S(2)}, u32[]{:S(2)}) collective-permute-start(f32[2,25,8,1]{3,1,2,0:T(8,128)S(1)} %get-tuple-element.43), channel_id=1, source_target_pairs={{0,16},{16,32},{32,48},{48,64},{64,80},{80,96},{96,112},{112,128},... | collective-permute-start | bytes 4808 | tf_op jit(solution)/shard_map/ppermute | solution.py:16
  27.7 7.1 %collective-permute-start.4 = (f32[2,25,8,1]{3,1,2,0:T(8,128)S(1)}, f32[2,25,8,1]{3,1,2,0:T(8,128)S(1)}, u32[]{:S(2)}, u32[]{:S(2)}) collective-permute-start(f32[2,25,8,1]{3,1,2,0:T(8,128)S(1)} %get-tuple-element.42), channel_id=1, source_target_pairs={{16,0},{32,16},{48,32},{64,48},{80,64},{96,80},{112,96},{128,112},... | collective-permute-start | bytes 4808 | tf_op jit(solution)/shard_map/ppermute | solution.py:18
  29.6 10.4 %collective-permute-start.5 = (f32[2,25,8,1]{3,1,2,0:T(8,128)S(1)}, f32[2,25,8,1]{3,1,2,0:T(8,128)S(1)}, u32[]{:S(2)}, u32[]{:S(2)}) collective-permute-start(f32[2,25,8,1]{3,1,2,0:T(8,128)S(1)} %get-tuple-element.41), channel_id=1, source_target_pairs={{0,16},{16,32},{32,48},{48,64},{64,80},{80,96},{96,112},{112,128},... | collective-permute-start | bytes 4808 | tf_op jit(solution)/shard_map/ppermute | solution.py:16
  40.5 7.1 %collective-permute-start.6 = (f32[2,25,8,1]{3,1,2,0:T(8,128)S(1)}, f32[2,25,8,1]{3,1,2,0:T(8,128)S(1)}, u32[]{:S(2)}, u32[]{:S(2)}) collective-permute-start(f32[2,25,8,1]{3,1,2,0:T(8,128)S(1)} %get-tuple-element.40), channel_id=1, source_target_pairs={{16,0},{32,16},{48,32},{64,48},{80,64},{96,80},{112,96},{128,112},... | collective-permute-start | bytes 4808 | tf_op jit(solution)/shard_map/ppermute | solution.py:18
  42.5 10.4 %collective-permute-start.7 = (f32[2,25,8,1]{3,1,2,0:T(8,128)S(1)}, f32[2,25,8,1]{3,1,2,0:T(8,128)S(1)}, u32[]{:S(2)}, u32[]{:S(2)}) collective-permute-start(f32[2,25,8,1]{3,1,2,0:T(8,128)S(1)} %get-tuple-element.39), channel_id=1, source_target_pairs={{0,16},{16,32},{32,48},{48,64},{64,80},{80,96},{96,112},{112,128},... | collective-permute-start | bytes 4808 | tf_op jit(solution)/shard_map/ppermute | solution.py:16
  53.4 7.1 %collective-permute-start.8 = (f32[2,25,8,1]{3,1,2,0:T(8,128)S(1)}, f32[2,25,8,1]{3,1,2,0:T(8,128)S(1)}, u32[]{:S(2)}, u32[]{:S(2)}) collective-permute-start(f32[2,25,8,1]{3,1,2,0:T(8,128)S(1)} %get-tuple-element.38), channel_id=1, source_target_pairs={{16,0},{32,16},{48,32},{64,48},{80,64},{96,80},{112,96},{128,112},... | collective-permute-start | bytes 4808 | tf_op jit(solution)/shard_map/ppermute | solution.py:18
  55.3 10.4 %collective-permute-start.9 = (f32[2,25,8,1]{3,1,2,0:T(8,128)S(1)}, f32[2,25,8,1]{3,1,2,0:T(8,128)S(1)}, u32[]{:S(2)}, u32[]{:S(2)}) collective-permute-start(f32[2,25,8,1]{3,1,2,0:T(8,128)S(1)} %get-tuple-element.37), channel_id=1, source_target_pairs={{0,16},{16,32},{32,48},{48,64},{64,80},{80,96},{96,112},{112,128},... | collective-permute-start | bytes 4808 | tf_op jit(solution)/shard_map/ppermute | solution.py:16
  69.0 30.0 %all-to-all-start = ((f32[16,1,4800]{2,1,0:T(1,128)}), f32[16,1,4800]{2,1,0:T(1,128)S(1)}, u32[]{:S(2)}, u32[]{:S(2)}) async-start(f32[16,1,4800]{2,1,0:T(1,128)} %reshape.185), calls=%async_computation | async-start | bytes 622592 | tf_op jit(solution)/shard_map/all_to_all | solution.py:113
  104.4 23.2 %copy-start.2 = (f32[128,1,200]{0,2,1:T(8,128)}, f32[128,1,200]{0,2,1:T(8,128)S(1)}, u32[]{:S(2)}) copy-start(f32[128,1,200]{0,2,1:T(8,128)S(1)} %get-tuple-element.31) | copy-start | bytes 307204
  186.6 21.8 %copy-start.3 = (f32[128,1,200]{0,2,1:T(8,128)S(1)}, f32[128,1,200]{0,2,1:T(8,128)}, u32[]{:S(2)}) copy-start(f32[128,1,200]{0,2,1:T(8,128)} %copy-done.2) | copy-start | bytes 307204
  191.0 22.6 %copy-start.5 = (f32[1,1,200]{0,2,1:T(8,128)S(1)}, f32[1,1,200]{0,2,1:T(8,128)}, u32[]{:S(2)}) copy-start(f32[1,1,200]{0,2,1:T(8,128)} %copy-done.4) | copy-start | bytes 2404
  191.0 22.6 %copy-start.7 = (f32[1,1,200]{0,2,1:T(8,128)S(1)}, f32[1,1,200]{0,2,1:T(8,128)}, u32[]{:S(2)}) copy-start(f32[1,1,200]{0,2,1:T(8,128)} %copy-done.6) | copy-start | bytes 2404
  191.0 22.6 %copy-start.9 = (f32[1,1,200]{0,2,1:T(8,128)S(1)}, f32[1,1,200]{0,2,1:T(8,128)}, u32[]{:S(2)}) copy-start(f32[1,1,200]{0,2,1:T(8,128)} %copy-done.8) | copy-start | bytes 2404
  191.0 22.6 %copy-start.11 = (f32[1,1,200]{0,2,1:T(8,128)S(1)}, f32[1,1,200]{0,2,1:T(8,128)}, u32[]{:S(2)}) copy-start(f32[1,1,200]{0,2,1:T(8,128)} %copy-done.10) | copy-start | bytes 2404
  192.1 21.5 %copy-start.44 = (f32[4,1,200]{0,2,1:T(8,128)S(1)}, f32[4,1,200]{0,2,1:T(8,128)}, u32[]{:S(2)}) copy-start(f32[4,1,200]{0,2,1:T(8,128)} %get-tuple-element.21) | copy-start | bytes 9604
  197.8 17.0 %copy-start.98 = (f32[2,1,200]{0,2,1:T(8,128)S(1)}, f32[2,1,200]{0,2,1:T(8,128)}, u32[]{:S(2)}) copy-start(f32[2,1,200]{0,2,1:T(8,128)} %get-tuple-element.138) | copy-start | bytes 4804
  253.1 15.4 %copy-start.54 = (f32[8,1,200]{0,2,1:T(8,128)S(1)}, f32[8,1,200]{0,2,1:T(8,128)}, u32[]{:S(2)}) copy-start(f32[8,1,200]{0,2,1:T(8,128)} %slice.870) | copy-start | bytes 19204
  253.1 16.1 %copy-start.29 = (f32[8,1,200]{0,2,1:T(8,128)S(1)}, f32[8,1,200]{0,2,1:T(8,128)}, u32[]{:S(2)}) copy-start(f32[8,1,200]{0,2,1:T(8,128)} %copy-done.28) | copy-start | bytes 19204
  253.8 15.5 %copy-start.31 = (f32[8,1,200]{0,2,1:T(8,128)S(1)}, f32[8,1,200]{0,2,1:T(8,128)}, u32[]{:S(2)}) copy-start(f32[8,1,200]{0,2,1:T(8,128)} %copy-done.30) | copy-start | bytes 19204
  255.2 15.3 %copy-start.60 = (f32[4,1,200]{0,2,1:T(8,128)S(1)}, f32[4,1,200]{0,2,1:T(8,128)}, u32[]{:S(2)}) copy-start(f32[4,1,200]{0,2,1:T(8,128)} %slice.886) | copy-start | bytes 9604
  (131 other events, 747.2 us)
where the time goes:
time: 315 us; the launch traced here: 309 us
  local copies, waits for them, and re-layouts  165 us (52%)
  starting transfers between devices  48.7 us (15%)
  waiting for transfers between devices  41.5 us (13%)
  other arithmetic  36.1 us (11%)
  blocking collectives  13.2 us (4%)
    slice x95, local copies, waits for them, and re-layouts, forward_local(): return lax.associative_scan(compose_forward, elements, axis=along)  93 us
    ppermute x5, waiting for transfers between devices, with_halo(): lax.ppermute(tail, axis, [(i, (i + 1) % count) for i in range(count)])  21.8 us
    pad x36, local copies, waits for them, and re-layouts, forward_local(): return lax.associative_scan(compose_forward, elements, axis=along)  17.9 us
    all_to_all x1, starting transfers between devices, per_device(): lax.all_to_all(stacked, 'lat', split_axis=3, concat_axis=2, tiled=True)  17.4 us
    slice x29, local copies, waits for them, and re-layouts, backward_local(): scanned = lax.associative_scan(compose_backward, flipped, axis=along)  16.1 us
    ppermute x5, starting transfers between devices, with_halo(): lax.ppermute(tail, axis, [(i, (i + 1) % count) for i in range(count)])  16 us
    ppermute x5, starting transfers between devices, with_halo(): lax.ppermute(head, axis, [((i + 1) % count, i) for i in range(count)])  15.3 us
    all_to_all x1, blocking collectives, solve_columns(): lax.all_to_all(solved_cols, 'lat', split_axis=2, concat_axis=3, tiled=True)  13.2 us
  transfers between devices with their start and end apart: 11, of which 9 were waited for; matrix products, arithmetic and copies ran while one was open for 1% of the time, Pallas kernels for 0%

commit v1 on v0

v1 whole, which is shorter than its diff:
```python
import functools

import jax
import jax.numpy as jnp
from jax import lax
from jax.experimental import pallas as pl
from jax.experimental.pallas import tpu as pltpu
from jax.sharding import PartitionSpec as P

LEV = 25
FIELDS = 2
STEPS = 4
ROWS = 8
LANES = 128
HALF = 13
PAD = HALF + 16
MESH = pl.DeviceIdType.MESH
F32 = jnp.float32
BF16 = jnp.bfloat16


def roll(cells, shift):
    return pltpu.roll(cells, shift % LANES, axis=cells.ndim - 1)


def by_level(ref, half, row):
    return ref[pl.ds(half * HALF * ROWS + row, 16, stride=ROWS), :]


def diffuse(state, face_east, face_west):
    for _ in range(STEPS):
        state = state + (
            face_east * (roll(state, -1) - state) - face_west * (state - roll(state, 1))
        )
    return state


def kernel(
    n_lon, n_lat,
    tr_h, mk_h, kl_h, kt_h, vr_h, out,
    tr, mk, kl, kt, vr,
    lon_s, halo_out, halo_in, inner, lat_s, diff_s, ocean_s,
    ratio_s, ipiv_s, g1_s, g8_s, part_s,
    msg_g, got_g, msg_p, got_p, msg_f, got_f, twice_s, vpad, x_s,
    in_sem, halo_ss, halo_rs, g_ss, g_rs, p_ss, p_rs, f_ss, f_rs,
):
    lon, lat = lax.axis_index("lon"), lax.axis_index("lat")
    east, west = lax.rem(lon + 1, n_lon), lax.rem(lon + n_lon - 1, n_lon)
    solver = lat < HALF

    loads = [
        pltpu.make_async_copy(src, dst, in_sem.at[i])
        for i, (src, dst) in enumerate(
            ((mk_h, mk), (kl_h, kl), (tr_h, tr), (kt_h, kt), (vr_h, vr))
        )
    ]
    for load in loads:
        load.start()

    barrier = pltpu.get_barrier_semaphore()
    for side in (east, west):
        pl.semaphore_signal(barrier, inc=1, device_id={"lon": side}, device_id_type=MESH)

    @pl.loop(1, n_lat)
    def _(d):
        pl.semaphore_signal(
            barrier, inc=1, device_id={"lat": lax.rem(lat + d, n_lat)}, device_id_type=MESH
        )

    lane = lax.broadcasted_iota(jnp.int32, (ROWS, LANES), 1)
    group = lane >> 4
    slot = (lane >> 2) & 3

    def pick(mask, yes, no):
        return jnp.where(jnp.broadcast_to(mask, yes.shape), yes, no)

    got_f[pl.ds(HALF * ROWS, 3 * ROWS), :] = jnp.zeros((3 * ROWS, LANES), F32)
    vpad[...] = jnp.zeros(vpad.shape, F32)
    lat_s[pl.ds(LEV * ROWS, (PAD - LEV) * ROWS), :] = jnp.zeros(((PAD - LEV) * ROWS, LANES), F32)
    for f in range(FIELDS):
        diff_s[f, pl.ds(LEV * ROWS, (PAD - LEV) * ROWS), :] = jnp.zeros(
            ((PAD - LEV) * ROWS, LANES), F32
        )

    loads[0].wait()
    loads[1].wait()
    loads[2].wait()
    for t in range(4):
        n = min(ROWS, LEV - ROWS * t)
        levels = pl.ds(ROWS * t, n)
        ocean = mk[levels].astype(F32)
        ocean_s[pl.ds(ROWS * ROWS * t, n * ROWS), :] = ocean.reshape(n * ROWS, LANES)
        lon_s[0, t, pl.ds(0, n)] = kl[levels].astype(F32) * ocean
        for f in range(FIELDS):
            lon_s[1 + f, t, pl.ds(0, n)] = tr[f, levels] * ocean
    edges = roll(lon_s[:, 0:3, 0], 8)
    for g in range(1, 8):
        edges = pick(group == g, roll(lon_s[:, 0:3, g], 16 * g + 8), edges)
    packed = [edges[:, 0], edges[:, 1], edges[:, 2], roll(lon_s[:, 3, 0], 8)]
    to_east, to_west = roll(packed[0], -4), roll(packed[0], -8)
    for t in range(1, 4):
        to_east = pick(slot == t, roll(packed[t], 4 * t - 4), to_east)
        to_west = pick(slot == t, roll(packed[t], 4 * t - 8), to_west)
    halo_out[0] = to_east
    halo_out[1] = to_west

    pl.semaphore_wait(barrier, n_lat + 1)
    halos = [
        pltpu.make_async_remote_copy(
            src_ref=halo_out.at[i], dst_ref=halo_in.at[i],
            send_sem=halo_ss.at[i], recv_sem=halo_rs.at[i],
            device_id={"lon": side}, device_id_type=MESH,
        )
        for i, side in enumerate((east, west))
    ]
    for halo in halos:
        halo.start()

    loads[3].wait()
    lat_s[pl.ds(0, LEV * ROWS), :] = kt[...].astype(F32).reshape(LEV * ROWS, LANES) * ocean_s[...]
    coef = [jnp.stack([by_level(lat_s, h, y) for h in range(2)]) for y in range(ROWS)]
    ones = jnp.ones_like(coef[0])
    excess = jnp.zeros_like(ones)
    ratio, ipiv, first = [], [], [ones]
    for y in range(ROWS):
        if y < ROWS - 1:
            face = jnp.minimum(coef[y], coef[y + 1])
            inverse = 1.0 / (1.0 + face + excess)
            ratio.append(face * inverse)
            excess = ratio[y] * (1.0 + excess)
            first.append(ratio[y] * first[y])
            ratio_s[y] = ratio[y]
        else:
            inverse = 1.0 / (1.0 + excess)
        ipiv.append(inverse)
        ipiv_s[y] = inverse
    g1, g8 = first[ROWS - 1] * ipiv[ROWS - 1], ipiv[ROWS - 1]
    g88 = g8
    g1_s[ROWS - 1], g8_s[ROWS - 1] = g1, g8
    for y in reversed(range(ROWS - 1)):
        g1 = first[y] * ipiv[y] + ratio[y] * g1
        g8 = ratio[y] * g8
        g1_s[y], g8_s[y] = g1, g8
    for h in range(2):
        for f in range(FIELDS):
            for q, value in enumerate((g1, g88, g8)):
                msg_g[pl.ds(4 * q + 2 * f + h, HALF, stride=16), :] = value[h, :HALF]
        msg_g[pl.ds(12 + h, HALF, stride=16), :] = coef[0][h, :HALF]
        msg_g[pl.ds(14 + h, HALF, stride=16), :] = coef[ROWS - 1][h, :HALF]

    def rows_of(ref, at, count):
        return ref.at[pl.ds(pl.multiple_of(at * count, count), count)]

    def to_solver(msg, got, count, ss, rs, k):
        return pltpu.make_async_remote_copy(
            src_ref=rows_of(msg, k, count), dst_ref=rows_of(got, lat, count),
            send_sem=ss, recv_sem=rs, device_id={"lat": k}, device_id_type=MESH,
        )

    def send_to_solvers(msg, got, count, ss, rs):
        @pl.loop(1, n_lat)
        def _(d):
            k = lax.rem(lat + d, n_lat)

            @pl.when(k < HALF)
            def _():
                to_solver(msg, got, count, ss, rs, k).start()

        @pl.when(solver)
        def _():
            at = pl.ds(pl.multiple_of(lat * count, count), count)
            got[at, :] = msg[at, :]

    def total(ref, rows, ss, rs):
        return pltpu.make_async_remote_copy(
            src_ref=ref.at[pl.ds(0, rows)], dst_ref=ref.at[pl.ds(0, rows)],
            send_sem=ss, recv_sem=rs, device_id={"lat": lax.rem(lat + 1, n_lat)}, device_id_type=MESH,
        )

    send_to_solvers(msg_g, got_g, 16, g_ss, g_rs)

    for t in range(4):
        n = min(ROWS, LEV - ROWS * t)
        coefs = lon_s[0, t, pl.ds(0, n)]
        face_east = jnp.minimum(coefs, roll(coefs, -1))
        face_west = roll(face_east, 1)
        for f in range(FIELDS):
            inner[f, t, pl.ds(0, n)] = diffuse(lon_s[1 + f, t, pl.ds(0, n)], face_east, face_west)

    for halo in halos:
        halo.wait_recv()
    from_west, from_east = halo_in[0], halo_in[1]
    for t in range(4):
        at_west = pick(slot == 1, roll(from_west, 4 - 4 * t), packed[t])
        at_east = pick(slot == 2, roll(from_east, 8 - 4 * t), packed[t])
        done = []
        for side in (at_west, at_east):
            face_east = jnp.minimum(side[0], roll(side[0], -1))
            done.append(diffuse(side[1:], face_east, roll(face_east, 1)))
        both = pick((lane & 15) < 8, done[1], done[0])
        for g in range(min(ROWS, LEV - ROWS * t)):
            whole = pick(
                (lane < 4) | (lane >= 124), roll(both, -16 * g - 8), inner[:, t, g]
            )
            for f in range(FIELDS):
                diff_s[f, pl.ds((ROWS * t + g) * ROWS, ROWS), :] = whole[f]

    for f in range(FIELDS):
        for h in range(2):
            p1 = p8 = jnp.zeros((16, LANES), F32)
            for y in range(ROWS):
                value = by_level(diff_s.at[f], h, y)
                p1 = p1 + g1_s[y, h] * value
                p8 = p8 + g8_s[y, h] * value
            msg_p[pl.ds(2 * f + h, HALF, stride=ROWS), :] = p1[:HALF]
            msg_p[pl.ds(4 + 2 * f + h, HALF, stride=ROWS), :] = p8[:HALF]
    send_to_solvers(msg_p, got_p, ROWS, p_ss, p_rs)

    for f in range(FIELDS):
        for h in range(2):
            values = [by_level(diff_s.at[f], h, y) for y in range(ROWS)]
            for y in range(1, ROWS):
                values[y] = values[y] + ratio_s[y - 1, h] * values[y - 1]
            local = values[ROWS - 1] * ipiv_s[ROWS - 1, h]
            part_s[f, h, ROWS - 1] = local
            for y in reversed(range(ROWS - 1)):
                local = values[y] * ipiv_s[y, h] + ratio_s[y, h] * local
                part_s[f, h, y] = local
    loads[4].wait()
    col = lax.broadcasted_iota(jnp.int32, (32, LANES), 1)
    weights = []
    for f in range(FIELDS):
        vpad[f, 0:LEV, 0:LEV] = vr[:, f, :]
        root = vpad[f]
        root = jnp.where(col < HALF, root, 0.0) + jnp.where((col >= 16) & (col < 28), roll(root, 3), 0.0)
        high = root.astype(BF16)
        low = (root - high.astype(F32)).astype(BF16)
        stacked = jnp.concatenate([high.astype(F32), low.astype(F32)], axis=0)
        weights.append((stacked + roll(stacked, 32)).astype(BF16)[:, :64])

    @pl.when(solver)
    def _():
        total(got_g, (n_lat - 1) * 16, g_ss, g_rs).wait_recv()
        block = [got_g.at[pl.ds(16 * b, 16)] for b in range(n_lat)]
        for m in range(n_lat - 1):
            u = jnp.minimum(block[m][14:16, :], block[m + 1][12:14, :])
            twice_s[m, 0:2] = u
            twice_s[m, 2:4] = u
        gamma = jnp.zeros((4, LANES), F32)
        alphas, betas, gammas = [], [], []
        for m in range(n_lat - 1):
            u = twice_s[m]
            low, up = block[m][8:12, :], block[m + 1][8:12, :]
            own = block[m + 1][0:4, :] + (block[m][4:8, :] - low * gamma)
            beta = u / (1.0 + u * own)
            gamma = beta * up
            alphas.append(beta * low)
            betas.append(beta)
            gammas.append(gamma)
        total(got_p, (n_lat - 1) * ROWS, p_ss, p_rs).wait_recv()
        flux = jnp.zeros((4, LANES), F32)
        reduced = []
        for m in range(n_lat - 1):
            jump = got_p[ROWS * (m + 1) : ROWS * (m + 1) + 4, :] - got_p[ROWS * m + 4 : ROWS * m + 8, :]
            flux = betas[m] * jump + alphas[m] * flux
            reduced.append(flux)
        flux = jnp.zeros((4, LANES), F32)
        msg_f[ROWS * n_lat - 4 : ROWS * n_lat, :] = flux
        msg_f[0:4, :] = flux
        for m in reversed(range(n_lat - 1)):
            flux = reduced[m] + gammas[m] * flux
            msg_f[ROWS * m + 4 : ROWS * m + 8, :] = flux
            msg_f[ROWS * m + 8 : ROWS * m + 12, :] = flux

        @pl.loop(1, n_lat)
        def _(d):
            to_solver(msg_f, got_f, ROWS, f_ss, f_rs, lax.rem(lat + d, n_lat)).start()

        at = pl.ds(pl.multiple_of(lat * ROWS, ROWS), ROWS)
        got_f[at, :] = msg_f[at, :]
        total(got_f, (HALF - 1) * ROWS, f_ss, f_rs).wait_recv()

    @pl.when(jnp.logical_not(solver))
    def _():
        total(got_f, HALF * ROWS, f_ss, f_rs).wait_recv()

    for f in range(FIELDS):
        for h in range(2):
            down = got_f[pl.ds(2 * f + h, 16, stride=ROWS), :]
            up = got_f[pl.ds(4 + 2 * f + h, 16, stride=ROWS), :]
            for y in range(ROWS):
                solved = part_s[f, h, y] + (up * g8_s[y, h] - down * g1_s[y, h])
                high = solved.astype(BF16)
                x_s[f, 16 * h : 16 * h + 16, LANES * y : LANES * (y + 1)] = high
                x_s[f, 32 + 16 * h : 48 + 16 * h, LANES * y : LANES * (y + 1)] = (
                    solved - high.astype(F32)
                ).astype(BF16)
        mixed = jnp.dot(weights[f], x_s[f], preferred_element_type=F32)
        mixed = mixed[0:32] + mixed[32:64]
        for y in range(ROWS):
            rows = pl.ds(y, LEV, stride=ROWS)
            out[f, rows, :] = mixed[0:LEV, LANES * y : LANES * (y + 1)] * ocean_s[rows, :]

    for halo in halos:
        halo.wait_send()

    @pl.when(solver)
    def _():
        total(msg_g, (HALF - 1) * 16, g_ss, g_rs).wait_send()
        total(msg_p, (HALF - 1) * ROWS, p_ss, p_rs).wait_send()
        total(msg_f, (n_lat - 1) * ROWS, f_ss, f_rs).wait_send()

    @pl.when(jnp.logical_not(solver))
    def _():
        total(msg_g, HALF * 16, g_ss, g_rs).wait_send()
        total(msg_p, HALF * ROWS, p_ss, p_rs).wait_send()


def solution(mesh):
    n_lon, n_lat = mesh.shape["lon"], mesh.shape["lat"]

    def per_device(tracer, ocean_mask, kappa_lon, kappa_lat, vertical_root):
        cells = (LEV, ROWS, LANES)
        tiles = (ROWS, 2, 16, LANES)
        made = pl.pallas_call(
            functools.partial(kernel, n_lon, n_lat),
            out_shape=jax.ShapeDtypeStruct((FIELDS, LEV * ROWS, LANES), F32),
            in_specs=[pl.BlockSpec(memory_space=pltpu.HBM)] * 5,
            out_specs=pl.BlockSpec(memory_space=pltpu.VMEM),
            scratch_shapes=[
                pltpu.VMEM((FIELDS,) + cells, F32),
                pltpu.VMEM(cells, jnp.int32),
                pltpu.VMEM(cells, BF16),
                pltpu.VMEM(cells, BF16),
                pltpu.VMEM((LEV, FIELDS, LEV), F32),
                pltpu.VMEM((1 + FIELDS, 4, 8, ROWS, LANES), F32),
                pltpu.VMEM((2, 1 + FIELDS, ROWS, LANES), F32),
                pltpu.VMEM((2, 1 + FIELDS, ROWS, LANES), F32),
                pltpu.VMEM((FIELDS, 4, 8, ROWS, LANES), F32),
                pltpu.VMEM((PAD * ROWS, LANES), F32),
                pltpu.VMEM((FIELDS, PAD * ROWS, LANES), F32),
                pltpu.VMEM((LEV * ROWS, LANES), F32),
                pltpu.VMEM(tiles, F32),
                pltpu.VMEM(tiles, F32),
                pltpu.VMEM(tiles, F32),
                pltpu.VMEM(tiles, F32),
                pltpu.VMEM((FIELDS, 2, ROWS, 16, LANES), F32),
                pltpu.VMEM((HALF * 16, LANES), F32),
                pltpu.VMEM((n_lat * 16, LANES), F32),
                pltpu.VMEM((HALF * ROWS, LANES), F32),
                pltpu.VMEM((n_lat * ROWS, LANES), F32),
                pltpu.VMEM((n_lat * ROWS, LANES), F32),
                pltpu.VMEM((16 * ROWS, LANES), F32),
                pltpu.VMEM((n_lat - 1, 4, LANES), F32),
                pltpu.VMEM((FIELDS, 32, LANES), F32),
                pltpu.VMEM((FIELDS, 64, ROWS * LANES), BF16),
                pltpu.SemaphoreType.DMA((5,)),
                pltpu.SemaphoreType.DMA((2,)),
                pltpu.SemaphoreType.DMA((2,)),
            ]
            + [pltpu.SemaphoreType.DMA] * 6,
            compiler_params=pltpu.CompilerParams(
                collective_id=0, has_side_effects=True, vmem_limit_bytes=60 * 1024 * 1024
            ),
        )(tracer, ocean_mask, kappa_lon, kappa_lat, jnp.moveaxis(vertical_root, 0, 1))
        return made.reshape(FIELDS, LEV, ROWS, LANES)

    placed = (
        P(None, None, "lat", "lon"),
        P(None, "lat", "lon"),
        P(None, "lat", "lon"),
        P(None, "lat", "lon"),
        P(),
    )
    return jax.shard_map(
        per_device,
        mesh=mesh,
        in_specs=placed,
        out_specs=P(None, None, "lat", "lon"),
        check_vma=False,
    )
```

time: 315 us -> 31.8 us (0.10); the launches traced: 309 us -> 31.6 us
  local copies, waits for them, and re-layouts: 165 us -> 1.62 us
  starting transfers between devices: 48.7 us -> 0 us
  waiting for transfers between devices: 41.5 us -> 0 us
  other arithmetic: 36.1 us -> 0 us
  Pallas kernels: 0 us -> 30 us
  blocking collectives: 13.2 us -> 0 us
    slice x132 -> x0, local copies, waits for them, and re-layouts: 110 us -> none  [the longest x95 93 us: forward_local(): return lax.associative_scan(compose_forward, elements, axis=along)]
    ppermute x10 -> x0, starting transfers between devices: 31.3 us -> none  [the longest x5 16 us: with_halo(): lax.ppermute(tail, axis, [(i, (i + 1) % count) for i in range(count)])]
    pallas_call x0 -> x1, Pallas kernels: none -> 30 us  [per_device(): pl.pallas_call(functools.partial(kernel, n_lon, n_lat), out_shape=jax.Sha...]
    ppermute x10 -> x0, waiting for transfers between devices: 29 us -> none  [the longest x5 21.8 us: with_halo(): lax.ppermute(tail, axis, [(i, (i + 1) % count) for i in range(count)])]
    mul x47 -> x0, other arithmetic: 23.9 us -> none  [the longest x5 7.08 us: compose_forward(): decay * inverse]
    mul x65 -> x0, local copies, waits for them, and re-layouts: 21.3 us -> none  [the longest x11 7.81 us: compose_forward(): second_term * inverse]
    pad x48 -> x0, local copies, waits for them, and re-layouts: 21.2 us -> none  [the longest x36 17.9 us: forward_local(): return lax.associative_scan(compose_forward, elements, axis=along)]
    all_to_all x1 -> x0, starting transfers between devices: 17.4 us -> none  [per_device(): lax.all_to_all(stacked, 'lat', split_axis=3, concat_axis=2, tiled=True)]
  transfers between devices with their start and end apart: 11 -> 0, of which waited for: 9 -> 0; matrix products, arithmetic and copies ran while one was open for 1% -> 0% of each run, Pallas kernels for 0% -> 0%
where the time goes in v1:
time: 31.8 us; the launch traced here: 31.6 us
  Pallas kernels  30 us (94%)
  local copies, waits for them, and re-layouts  1.62 us (5%)
    pallas_call x1, Pallas kernels, per_device(): pl.pallas_call(functools.partial(kernel, n_lon, n_lat), out_shape=jax.Sha...  30 us
    unnamed x1, local copies, waits for them, and re-layouts  1.62 us

profile of v1, /device:TPU:1, one launch (start us, length us, event | category | flops | bytes accessed | tf_op | source)
XLA Modules:
  0.0 31.6 jit_solution(15169635655154642056)
XLA Ops:
  0.0 30.0 %shard_map.55 = f32[2,200,128]{2,1,0:T(8,128)} custom-call(f32[2,25,8,128]{3,2,1,0:T(8,128)} %tr_h.1, s32[25,8,128]{2,1,0:T(8,128)} %mk_h.1, bf16[25,8,128]{2,1,0:T(8,128)(2,1)} %kl_h.1, bf16[25,8,128]{2,1,0:T(8,128)(2,1)} %kt_h.1, f32[25,2,25]{2,1,0:T(2,128)} %bitcast.3), custom_call_target="tpu_custom_call" | custom-call | tf_op jit(solution)/shard_map/pallas_call | solution.py:325
  30.0 1.6 %copy.7 = f32[2,25,8,128]{3,2,1,0:T(8,128)} copy(f32[2,25,8,128]{3,2,1,0:T(8,128)} %bitcast.2) | data formatting | bytes 409600

commit v2 on v1

v2 whole, which is shorter than its diff:
```python
import functools

import jax
import jax.numpy as jnp
from jax import lax
from jax.experimental import pallas as pl
from jax.experimental.pallas import tpu as pltpu
from jax.sharding import PartitionSpec as P

LEV = 25
FIELDS = 2
STEPS = 4
ROWS = 8
LANES = 128
SOLVERS = 2
HALF = 13
PAD = HALF + 16
STARTS = (0, 8, 13, 21)
COUNTS = (8, 5, 8, 4)
MESH = pl.DeviceIdType.MESH
F32 = jnp.float32
BF16 = jnp.bfloat16


def roll(cells, shift):
    return pltpu.roll(cells, shift % LANES, axis=cells.ndim - 1)


def pick(mask, yes, no):
    return jnp.where(jnp.broadcast_to(mask, yes.shape), yes, no)


def by_level(ref, row):
    return jnp.stack(
        [ref[pl.ds(half * HALF * ROWS + row, 16, stride=ROWS), :] for half in range(2)]
    )


def by_row(ref, row):
    return ref[pl.ds(row, ROWS, stride=ROWS), :]


def diffuse(state, face_east, face_west):
    for _ in range(STEPS):
        state = state + (
            face_east * (roll(state, -1) - state) - face_west * (state - roll(state, 1))
        )
    return state


def factor(coef):
    ones = jnp.ones_like(coef[0])
    excess = jnp.zeros_like(ones)
    ratio, ipiv, first = [], [], [ones]
    for y in range(ROWS - 1):
        face = jnp.minimum(coef[y], coef[y + 1])
        ipiv.append(1.0 / (1.0 + face + excess))
        ratio.append(face * ipiv[y])
        excess = ratio[y] * (1.0 + excess)
        first.append(ratio[y] * first[y])
    ipiv.append(1.0 / (1.0 + excess))
    g1, g8 = [first[-1] * ipiv[-1]], [ipiv[-1]]
    for y in reversed(range(ROWS - 1)):
        g1.append(first[y] * ipiv[y] + ratio[y] * g1[-1])
        g8.append(ratio[y] * g8[-1])
    return ratio, ipiv, g1[::-1], g8[::-1]


def kernel(
    n_lon, n_lat,
    tr_h, mk_h, kl_h, kt_h, vr_h, out,
    tr, mk, kl, kt, vr,
    lon_s, halo_out, halo_in, lat_s, diff_s, ocean_s,
    ratio_s, ipiv_s, g1_s, g8_s, part_s, edge_c, edge_s, edge_g1, edge_g8,
    msg_g, got_g, msg_p, got_p, msg_f, got_f,
    msg_ge, got_ge, msg_pe, got_pe, msg_fe, got_fe,
    line_s, line_e, flux_s, vpad, x_s,
    in_sem, halo_ss, halo_rs, g_ss, g_rs, p_ss, p_rs, f_ss, f_rs, e_ss, e_rs,
):
    lon, lat = lax.axis_index("lon"), lax.axis_index("lat")
    east, west = lax.rem(lon + 1, n_lon), lax.rem(lon + n_lon - 1, n_lon)
    solver = lat < SOLVERS

    loads = [
        pltpu.make_async_copy(src, dst, in_sem.at[i])
        for i, (src, dst) in enumerate(
            ((mk_h, mk), (kl_h, kl), (tr_h, tr), (kt_h, kt), (vr_h, vr))
        )
    ]
    for load in loads:
        load.start()

    barrier = pltpu.get_barrier_semaphore()
    pl.semaphore_signal(barrier, inc=1, device_id={"lon": west}, device_id_type=MESH)

    @pl.when(solver)
    def _():
        @pl.loop(1, n_lat)
        def _(d):
            pl.semaphore_signal(
                barrier, inc=1, device_id={"lat": lax.rem(lat + d, n_lat)}, device_id_type=MESH
            )

    lane = lax.broadcasted_iota(jnp.int32, (ROWS, LANES), 1)
    slot = (lane >> 2) & 3
    group = lane >> 4
    edge = (lane < 4) | (lane >= LANES - 4)

    flux_s[...] = jnp.zeros(flux_s.shape, F32)
    vpad[...] = jnp.zeros(vpad.shape, F32)
    spare = pl.ds(LEV * ROWS, (PAD - LEV) * ROWS)
    lat_s[spare, :] = jnp.zeros(((PAD - LEV) * ROWS, LANES), F32)
    for f in range(FIELDS):
        diff_s[f, spare, :] = jnp.zeros(((PAD - LEV) * ROWS, LANES), F32)

    loads[0].wait()
    loads[1].wait()
    loads[2].wait()
    packed = []
    for t in range(4):
        n = COUNTS[t]
        levels = pl.ds(STARTS[t], n)
        ocean = mk[levels].astype(F32)
        ocean_s[pl.ds(STARTS[t] * ROWS, n * ROWS), :] = ocean.reshape(n * ROWS, LANES)
        lon_s[0, t, pl.ds(0, n)] = kl[levels].astype(F32) * ocean
        for f in range(FIELDS):
            lon_s[1 + f, t, pl.ds(0, n)] = tr[f, levels] * ocean
        tile = roll(lon_s[:, t, 0], 8)
        for g in range(1, n):
            tile = pick(group == 8 - g, roll(lon_s[:, t, g], 8 - 16 * g), tile)
        packed.append(tile)
    to_east, to_west = roll(packed[0], -4), roll(packed[0], -8)
    for t in range(1, 4):
        to_east = pick(slot == t, roll(packed[t], 4 * t - 4), to_east)
        to_west = pick(slot == t, roll(packed[t], 4 * t - 8), to_west)
    halo_out[0] = to_east
    halo_out[1] = to_west
    halos = [
        pltpu.make_async_remote_copy(
            src_ref=halo_out.at[i], dst_ref=halo_in.at[i],
            send_sem=halo_ss.at[i], recv_sem=halo_rs.at[i],
            device_id={"lon": side}, device_id_type=MESH,
        )
        for i, side in enumerate((east, west))
    ]

    @pl.when(solver)
    def _():
        pl.semaphore_wait(barrier, SOLVERS)

    @pl.when(jnp.logical_not(solver))
    def _():
        pl.semaphore_wait(barrier, SOLVERS + 1)

    halos[0].start()

    def to_solver(msg, got, h, ss, rs):
        return pltpu.make_async_remote_copy(
            src_ref=msg, dst_ref=got.at[lat], send_sem=ss.at[h], recv_sem=rs.at[h],
            device_id={"lat": h}, device_id_type=MESH,
        )

    def of_solver(msg, got, h, k, ss, rs):
        return pltpu.make_async_remote_copy(
            src_ref=msg.at[k], dst_ref=got, send_sem=ss.at[h], recv_sem=rs.at[h],
            device_id={"lat": k}, device_id_type=MESH,
        )

    def send(h, msg, got, ss, rs):
        @pl.when(lat != h)
        def _():
            to_solver(msg, got, h, ss, rs).start()

        @pl.when(lat == h)
        def _():
            got[lat] = msg[...]

    loads[3].wait()
    lat_s[pl.ds(0, LEV * ROWS), :] = kt[...].astype(F32).reshape(LEV * ROWS, LANES) * ocean_s[...]
    coef = [by_level(lat_s, y) for y in range(ROWS)]
    ratio, ipiv, g1, g8 = factor(coef)
    for y in range(ROWS):
        ipiv_s[y], g1_s[y], g8_s[y] = ipiv[y], g1[y], g8[y]
        if y < ROWS - 1:
            ratio_s[y] = ratio[y]
    for h in range(SOLVERS):
        for q, value in enumerate((g1[0], g8[-1], g8[0], coef[0], coef[-1])):
            msg_g[h, q] = value[h, :HALF]
    for t in range(4):
        tile = roll(lat_s[pl.ds(STARTS[t] * ROWS, ROWS), :], 8)
        for g in range(1, COUNTS[t]):
            tile = pick(
                group == 8 - g, roll(lat_s[pl.ds((STARTS[t] + g) * ROWS, ROWS), :], 8 - 16 * g), tile
            )
        for f in range(FIELDS):
            edge_c[pl.ds((4 * f + t) * ROWS, ROWS), :] = tile
    coef = [by_row(edge_c, y) for y in range(ROWS)]
    unused, unused, g1, g8 = factor(coef)
    for y in range(ROWS):
        edge_g1[y], edge_g8[y] = g1[y], g8[y]
    for q, value in enumerate((g1[0], g8[-1], g8[0], coef[0], coef[-1])):
        msg_ge[q] = value[0:4]
    for h in range(SOLVERS):
        send(h, msg_g.at[h], got_g, g_ss, g_rs)
    send(1, msg_ge, got_ge, e_ss.at[0], e_rs.at[0])

    halos[0].wait_recv()
    halos[1].start()

    for t in range(4):
        n = COUNTS[t]
        coefs = lon_s[0, t, pl.ds(0, n)]
        face_east = jnp.minimum(coefs, roll(coefs, -1))
        face_west = roll(face_east, 1)
        for f in range(FIELDS):
            diff_s[f, pl.ds(STARTS[t] * ROWS, n * ROWS), :] = diffuse(
                lon_s[1 + f, t, pl.ds(0, n)], face_east, face_west
            ).reshape(n * ROWS, LANES)
    for f in range(FIELDS):
        p1 = p8 = jnp.zeros((2, 16, LANES), F32)
        for y in range(ROWS):
            value = by_level(diff_s.at[f], y)
            p1 = p1 + g1_s[y] * value
            p8 = p8 + g8_s[y] * value
        for h in range(SOLVERS):
            msg_p[h, 2 * f] = p1[h, :HALF]
            msg_p[h, 2 * f + 1] = p8[h, :HALF]
    for h in range(SOLVERS):
        send(h, msg_p.at[h], got_p, p_ss, p_rs)

    halos[1].wait_recv()
    from_west, from_east = halo_in[0], halo_in[1]
    edges = []
    for t in range(4):
        at_west = pick(slot == 1, roll(from_west, 4 - 4 * t), packed[t])
        at_east = pick(slot == 2, roll(from_east, 8 - 4 * t), packed[t])
        done = []
        for side in (at_west, at_east):
            face_east = jnp.minimum(side[0], roll(side[0], -1))
            done.append(diffuse(side[1:], face_east, roll(face_east, 1)))
        edges.append(pick((lane & 15) < 8, done[1], done[0]))
        for f in range(FIELDS):
            edge_s[pl.ds((4 * f + t) * ROWS, ROWS), :] = edges[t][f]
    p1 = p8 = jnp.zeros((ROWS, LANES), F32)
    for y in range(ROWS):
        value = by_row(edge_s, y)
        p1 = p1 + edge_g1[y] * value
        p8 = p8 + edge_g8[y] * value
    msg_pe[0] = p1
    msg_pe[1] = p8
    send(1, msg_pe, got_pe, e_ss.at[1], e_rs.at[1])

    for t in range(4):
        for g in range(COUNTS[t]):
            rows = pl.ds((STARTS[t] + g) * ROWS, ROWS)
            ends = roll(edges[t], 16 * g - 8)
            for f in range(FIELDS):
                diff_s[f, rows, :] = jnp.where(edge, ends[f], diff_s[f, rows, :])
    for f in range(FIELDS):
        values = [by_level(diff_s.at[f], y) for y in range(ROWS)]
        for y in range(1, ROWS):
            values[y] = values[y] + ratio_s[y - 1] * values[y - 1]
        local = values[ROWS - 1] * ipiv_s[ROWS - 1]
        part_s[f, ROWS - 1] = local
        for y in reversed(range(ROWS - 1)):
            local = values[y] * ipiv_s[y] + ratio_s[y] * local
            part_s[f, y] = local
    loads[4].wait()
    col = lax.broadcasted_iota(jnp.int32, (32, LANES), 1)
    weights = []
    for f in range(FIELDS):
        vpad[f, 0:LEV, 0:LEV] = vr[:, f, :]
        root = vpad[f]
        root = jnp.where(col < HALF, root, 0.0) + jnp.where(
            (col >= 16) & (col < 16 + LEV - HALF), roll(root, 16 - HALF), 0.0
        )
        high = root.astype(BF16).astype(F32)
        stacked = jnp.concatenate([high, root - high], axis=0)
        weights.append((stacked + roll(stacked, 32)).astype(BF16)[:, :64])

    def total(ref, ss, rs):
        return pltpu.make_async_remote_copy(
            src_ref=ref, dst_ref=ref, send_sem=ss, recv_sem=rs,
            device_id={"lat": lax.rem(lat + 1, n_lat)}, device_id_type=MESH,
        )

    others = pl.ds(0, n_lat - 1)

    def lines(block, shape, keep):
        gamma = jnp.zeros(shape, F32)
        for m in range(n_lat - 1):
            u = jnp.minimum(block(m, 4), block(m + 1, 3))
            low = block(m, 2)
            own = block(m + 1, 0) + (block(m, 1) - low * gamma)
            beta = u / (1.0 + u * own)
            gamma = beta * block(m + 1, 2)
            for q, value in enumerate((beta, beta * low, gamma)):
                keep[m, q] = value

    def fluxes(jump, line, shape, put):
        flux = jnp.zeros(shape, F32)
        reduced = []
        for m in range(n_lat - 1):
            flux = line(m, 0) * jump(m) + line(m, 1) * flux
            reduced.append(flux)
        flux = jnp.zeros(shape, F32)
        put(n_lat - 1, 1, flux)
        put(0, 0, flux)
        for m in reversed(range(n_lat - 1)):
            flux = reduced[m] + line(m, 2) * flux
            put(m, 1, flux)
            put(m + 1, 0, flux)

    for h in range(SOLVERS):

        @pl.when(lat == h)
        def _():
            total(got_g.at[others], g_ss.at[h], g_rs.at[h]).wait_recv()
            lines(lambda b, q: got_g[b, q], (HALF, LANES), line_s)
            if h == 1:
                total(got_ge.at[others], e_ss.at[0, h], e_rs.at[0, h]).wait_recv()
                for e in range(2):
                    lines(lambda b, q: got_ge[b, q], (4, LANES), line_e.at[:, :, pl.ds(4 * e, 4)])
            total(got_p.at[others], p_ss.at[h], p_rs.at[h]).wait_recv()
            for f in range(FIELDS):

                def put(b, end, flux):
                    msg_f[b, 2 * f + end] = flux

                fluxes(
                    lambda m: got_p[m + 1, 2 * f] - got_p[m, 2 * f + 1],
                    lambda m, q: line_s[m, q], (HALF, LANES), put,
                )

            @pl.loop(1, n_lat)
            def _(d):
                of_solver(msg_f, got_f.at[h], h, lax.rem(lat + d, n_lat), f_ss, f_rs).start()

            got_f[h] = msg_f[h]

    for h in range(SOLVERS):

        @pl.when(lat != h)
        def _():
            of_solver(msg_f, got_f.at[h], h, h, f_ss, f_rs).wait_recv()

        flux_s[h, :, 0:HALF] = got_f[h]

    @pl.when(lat == 1)
    def _():
        total(got_pe.at[others], e_ss.at[1, 1], e_rs.at[1, 1]).wait_recv()

        def put(b, end, flux):
            msg_fe[b, end] = flux

        fluxes(
            lambda m: got_pe[m + 1, 0] - got_pe[m, 1],
            lambda m, q: line_e[m, q], (ROWS, LANES), put,
        )

        @pl.loop(1, n_lat)
        def _(d):
            of_solver(msg_fe, got_fe, 1, lax.rem(lat + d, n_lat), e_ss.at[2], e_rs.at[2]).start()

        got_fe[...] = msg_fe[1]

    @pl.when(lat != 1)
    def _():
        of_solver(msg_fe, got_fe, 1, 1, e_ss.at[2], e_rs.at[2]).wait_recv()

    flux_e = roll(got_fe[...], -8)
    for f in range(FIELDS):
        for h in range(2):
            flux = []
            for end in range(2):
                tiles = []
                for a in range(2):
                    row = 4 * f + 2 * h + a
                    ends = pltpu.roll(
                        jnp.broadcast_to(flux_e[end, row : row + 1], (ROWS, LANES)),
                        0, axis=1, stride=16, stride_axis=0,
                    )
                    tiles.append(
                        jnp.where(edge, ends, flux_s[h, 2 * f + end, ROWS * a : ROWS * (a + 1)])
                    )
                flux.append(jnp.concatenate(tiles, axis=0))
            for y in range(ROWS):
                solved = part_s[f, y, h] + (flux[1] * g8_s[y, h] - flux[0] * g1_s[y, h])
                high = solved.astype(BF16)
                x_s[f, 16 * h : 16 * h + 16, LANES * y : LANES * (y + 1)] = high
                x_s[f, 32 + 16 * h : 48 + 16 * h, LANES * y : LANES * (y + 1)] = (
                    solved - high.astype(F32)
                ).astype(BF16)
        mixed = jnp.dot(weights[f], x_s[f], preferred_element_type=F32)
        mixed = mixed[0:32] + mixed[32:64]
        for y in range(ROWS):
            rows = pl.ds(y, LEV, stride=ROWS)
            out[f, rows, :] = mixed[0:LEV, LANES * y : LANES * (y + 1)] * ocean_s[rows, :]

    for halo in halos:
        halo.wait_send()
    for h in range(SOLVERS):

        @pl.when(lat != h)
        def _():
            to_solver(msg_g.at[h], got_g, h, g_ss, g_rs).wait_send()
            to_solver(msg_p.at[h], got_p, h, p_ss, p_rs).wait_send()
            if h == 1:
                to_solver(msg_ge, got_ge, h, e_ss.at[0], e_rs.at[0]).wait_send()
                to_solver(msg_pe, got_pe, h, e_ss.at[1], e_rs.at[1]).wait_send()

        @pl.when(lat == h)
        def _():
            total(msg_f.at[others], f_ss.at[h], f_rs.at[h]).wait_send()
            if h == 1:
                total(msg_fe.at[others], e_ss.at[2, h], e_rs.at[2, h]).wait_send()


def solution(mesh):
    n_lon, n_lat = mesh.shape["lon"], mesh.shape["lat"]

    def per_device(tracer, ocean_mask, kappa_lon, kappa_lat, vertical_root):
        cells = (LEV, ROWS, LANES)
        natural = (PAD * ROWS, LANES)
        rows = (ROWS, 2, 16, LANES)
        scratch = [
            (FIELDS,) + cells,
            (cells, jnp.int32),
            (cells, BF16),
            (cells, BF16),
            (LEV, FIELDS, LEV),
            (1 + FIELDS, 4, 8, ROWS, LANES),
            (2, 1 + FIELDS, ROWS, LANES),
            (2, 1 + FIELDS, ROWS, LANES),
            natural,
            (FIELDS,) + natural,
            (LEV * ROWS, LANES),
            rows, rows, rows, rows,
            (FIELDS,) + rows,
            (64, LANES), (64, LANES),
            (ROWS, ROWS, LANES), (ROWS, ROWS, LANES),
            (SOLVERS, 5, HALF, LANES), (n_lat, 5, HALF, LANES),
            (SOLVERS, 4, HALF, LANES), (n_lat, 4, HALF, LANES),
            (n_lat, 4, HALF, LANES), (SOLVERS, 4, HALF, LANES),
            (5, 4, LANES), (n_lat, 5, 4, LANES),
            (2, ROWS, LANES), (n_lat, 2, ROWS, LANES),
            (n_lat, 2, ROWS, LANES), (2, ROWS, LANES),
            (n_lat - 1, 3, HALF, LANES),
            (n_lat - 1, 3, ROWS, LANES),
            (SOLVERS, 4, 16, LANES),
            (FIELDS, 32, LANES),
            ((FIELDS, 64, ROWS * LANES), BF16),
        ]
        scratch = [
            pltpu.VMEM(*item) if isinstance(item[0], tuple) else pltpu.VMEM(item, F32)
            for item in scratch
        ]
        sems = [(5,), (2,), (2,)] + [(SOLVERS,)] * 6 + [(3, SOLVERS)] * 2
        made = pl.pallas_call(
            functools.partial(kernel, n_lon, n_lat),
            out_shape=pltpu.VMEM((FIELDS, LEV * ROWS, LANES), F32),
            in_specs=[pl.BlockSpec(memory_space=pltpu.HBM)] * 5,
            out_specs=pl.BlockSpec(memory_space=pltpu.VMEM),
            scratch_shapes=scratch + [pltpu.SemaphoreType.DMA(shape) for shape in sems],
            compiler_params=pltpu.CompilerParams(
                collective_id=0, has_side_effects=True, vmem_limit_bytes=60 * 1024 * 1024
            ),
        )(tracer, ocean_mask, kappa_lon, kappa_lat, jnp.moveaxis(vertical_root, 0, 1))
        return made.reshape(FIELDS, LEV, ROWS, LANES)

    placed = (
        P(None, None, "lat", "lon"),
        P(None, "lat", "lon"),
        P(None, "lat", "lon"),
        P(None, "lat", "lon"),
        P(),
    )
    return jax.shard_map(
        per_device,
        mesh=mesh,
        in_specs=placed,
        out_specs=P(None, None, "lat", "lon"),
        check_vma=False,
    )
```

time: 31.8 us -> 32 us (level)
  Pallas kernels: 30 us -> 31.1 us
  local copies, waits for them, and re-layouts: 1.62 us -> 0.68 us
    pallas_call x1, Pallas kernels: 30 us -> 31.1 us  [per_device(): pl.pallas_call(functools.partial(kernel, n_lon, n_lat), out_shape=pltpu.V...]
    unnamed x1, local copies, waits for them, and re-layouts: 1.62 us -> 0.68 us
where the time goes in v2:
time: 32 us; the launch traced here: 31.8 us
  Pallas kernels  31.1 us (97%)
  local copies, waits for them, and re-layouts  0.68 us (2%)
    pallas_call x1, Pallas kernels, per_device(): pl.pallas_call(functools.partial(kernel, n_lon, n_lat), out_shape=pltpu.V...  31.1 us
    unnamed x1, local copies, waits for them, and re-layouts  0.68 us

profile of v2, /device:TPU:1, one launch (start us, length us, event | category | flops | bytes accessed | tf_op | source)
XLA Modules:
  0.0 31.8 jit_solution(6643364384407729879)
XLA Ops:
  0.0 31.1 %shard_map.55 = f32[2,200,128]{2,1,0:T(8,128)S(1)} custom-call(f32[2,25,8,128]{3,2,1,0:T(8,128)} %tr_h.1, s32[25,8,128]{2,1,0:T(8,128)} %mk_h.1, bf16[25,8,128]{2,1,0:T(8,128)(2,1)} %kl_h.1, bf16[25,8,128]{2,1,0:T(8,128)(2,1)} %kt_h.1, f32[25,2,25]{2,1,0:T(2,128)} %bitcast.3), custom_call_target="tpu_custom_call" | custom-call | tf_op jit(solution)/shard_map/pallas_call | solution.py:459
  31.2 0.7 %copy.7 = f32[2,25,8,128]{3,2,1,0:T(8,128)} copy(f32[2,25,8,128]{3,2,1,0:T(8,128)S(1)} %bitcast.2) | data formatting | bytes 409600

commit v3 on v2

--- a/solution.py
+++ b/solution.py
@@ -12,8 +12,8 @@
 STEPS = 4
 ROWS = 8
 LANES = 128
-SOLVERS = 2
 HALF = 13
+ENDS = 1
 PAD = HALF + 16
 STARTS = (0, 8, 13, 21)
 COUNTS = (8, 5, 8, 4)
@@ -74,12 +74,12 @@
     ratio_s, ipiv_s, g1_s, g8_s, part_s, edge_c, edge_s, edge_g1, edge_g8,
     msg_g, got_g, msg_p, got_p, msg_f, got_f,
     msg_ge, got_ge, msg_pe, got_pe, msg_fe, got_fe,
-    line_s, line_e, flux_s, vpad, x_s,
+    line_s, line_e, vpad, x_s,
     in_sem, halo_ss, halo_rs, g_ss, g_rs, p_ss, p_rs, f_ss, f_rs, e_ss, e_rs,
 ):
     lon, lat = lax.axis_index("lon"), lax.axis_index("lat")
     east, west = lax.rem(lon + 1, n_lon), lax.rem(lon + n_lon - 1, n_lon)
-    solver = lat < SOLVERS
+    solver = lat < HALF
 
     loads = [
         pltpu.make_async_copy(src, dst, in_sem.at[i])
@@ -91,7 +91,8 @@
         load.start()
 
     barrier = pltpu.get_barrier_semaphore()
-    pl.semaphore_signal(barrier, inc=1, device_id={"lon": west}, device_id_type=MESH)
+    for side in (east, west):
+        pl.semaphore_signal(barrier, inc=1, device_id={"lon": side}, device_id_type=MESH)
 
     @pl.when(solver)
     def _():
@@ -106,7 +107,7 @@
     group = lane >> 4
     edge = (lane < 4) | (lane >= LANES - 4)
 
-    flux_s[...] = jnp.zeros(flux_s.shape, F32)
+    got_f[HALF:16] = jnp.zeros((16 - HALF, ROWS, LANES), F32)
     vpad[...] = jnp.zeros(vpad.shape, F32)
     spare = pl.ds(LEV * ROWS, (PAD - LEV) * ROWS)
     lat_s[spare, :] = jnp.zeros(((PAD - LEV) * ROWS, LANES), F32)
@@ -146,34 +147,60 @@
 
     @pl.when(solver)
     def _():
-        pl.semaphore_wait(barrier, SOLVERS)
+        pl.semaphore_wait(barrier, HALF + 1)
 
     @pl.when(jnp.logical_not(solver))
     def _():
-        pl.semaphore_wait(barrier, SOLVERS + 1)
-
-    halos[0].start()
-
-    def to_solver(msg, got, h, ss, rs):
+        pl.semaphore_wait(barrier, HALF + 2)
+
+    for halo in halos:
+        halo.start()
+
+    def tile_to(msg, got, ss, rs, k):
         return pltpu.make_async_remote_copy(
-            src_ref=msg, dst_ref=got.at[lat], send_sem=ss.at[h], recv_sem=rs.at[h],
-            device_id={"lat": h}, device_id_type=MESH,
-        )
-
-    def of_solver(msg, got, h, k, ss, rs):
+            src_ref=msg.at[k], dst_ref=got.at[lat],
+            send_sem=ss, recv_sem=rs, device_id={"lat": k}, device_id_type=MESH,
+        )
+
+    def send_to_solvers(msg, got, ss, rs):
+        @pl.loop(1, n_lat)
+        def _(d):
+            k = lax.rem(lat + d, n_lat)
+
+            @pl.when(k < HALF)
+            def _():
+                tile_to(msg, got, ss, rs, k).start()
+
+        @pl.when(solver)
+        def _():
+            got[lat] = msg[lat]
+
+    def total(ref, ss, rs):
         return pltpu.make_async_remote_copy(
-            src_ref=msg.at[k], dst_ref=got, send_sem=ss.at[h], recv_sem=rs.at[h],
+            src_ref=ref, dst_ref=ref, send_sem=ss, recv_sem=rs,
+            device_id={"lat": lax.rem(lat + 1, n_lat)}, device_id_type=MESH,
+        )
+
+    def to_ends(msg, got, i):
+        return pltpu.make_async_remote_copy(
+            src_ref=msg, dst_ref=got.at[lat], send_sem=e_ss.at[i], recv_sem=e_rs.at[i],
+            device_id={"lat": ENDS}, device_id_type=MESH,
+        )
+
+    def of_ends(k):
+        return pltpu.make_async_remote_copy(
+            src_ref=msg_fe.at[k], dst_ref=got_fe, send_sem=e_ss.at[2], recv_sem=e_rs.at[2],
             device_id={"lat": k}, device_id_type=MESH,
         )
 
-    def send(h, msg, got, ss, rs):
-        @pl.when(lat != h)
+    def send_to_ends(msg, got, i):
+        @pl.when(lat != ENDS)
         def _():
-            to_solver(msg, got, h, ss, rs).start()
-
-        @pl.when(lat == h)
+            to_ends(msg, got, i).start()
+
+        @pl.when(lat == ENDS)
         def _():
-            got[lat] = msg[...]
+            got[ENDS] = msg[...]
 
     loads[3].wait()
     lat_s[pl.ds(0, LEV * ROWS), :] = kt[...].astype(F32).reshape(LEV * ROWS, LANES) * ocean_s[...]
@@ -183,9 +210,10 @@
         ipiv_s[y], g1_s[y], g8_s[y] = ipiv[y], g1[y], g8[y]
         if y < ROWS - 1:
             ratio_s[y] = ratio[y]
-    for h in range(SOLVERS):
+    for h in range(2):
         for q, value in enumerate((g1[0], g8[-1], g8[0], coef[0], coef[-1])):
-            msg_g[h, q] = value[h, :HALF]
+            msg_g[:, 2 * q + h, :] = value[h, :HALF]
+    send_to_solvers(msg_g, got_g, g_ss, g_rs)
     for t in range(4):
         tile = roll(lat_s[pl.ds(STARTS[t] * ROWS, ROWS), :], 8)
         for g in range(1, COUNTS[t]):
@@ -200,12 +228,7 @@
         edge_g1[y], edge_g8[y] = g1[y], g8[y]
     for q, value in enumerate((g1[0], g8[-1], g8[0], coef[0], coef[-1])):
         msg_ge[q] = value[0:4]
-    for h in range(SOLVERS):
-        send(h, msg_g.at[h], got_g, g_ss, g_rs)
-    send(1, msg_ge, got_ge, e_ss.at[0], e_rs.at[0])
-
-    halos[0].wait_recv()
-    halos[1].start()
+    send_to_ends(msg_ge, got_ge, 0)
 
     for t in range(4):
         n = COUNTS[t]
@@ -222,13 +245,40 @@
             value = by_level(diff_s.at[f], y)
             p1 = p1 + g1_s[y] * value
             p8 = p8 + g8_s[y] * value
-        for h in range(SOLVERS):
-            msg_p[h, 2 * f] = p1[h, :HALF]
-            msg_p[h, 2 * f + 1] = p8[h, :HALF]
-    for h in range(SOLVERS):
-        send(h, msg_p.at[h], got_p, p_ss, p_rs)
-
-    halos[1].wait_recv()
+        for h in range(2):
+            msg_p[:, 2 * f + h, :] = p1[h, :HALF]
+            msg_p[:, 4 + 2 * f + h, :] = p8[h, :HALF]
+    send_to_solvers(msg_p, got_p, p_ss, p_rs)
+
+    others = n_lat - 1
+
+    def lines(face, own_first, own_last, cross, shape, keep):
+        gamma = jnp.zeros(shape, F32)
+        for m in range(others):
+            low = cross(m)
+            beta = face(m)
+            beta = beta / (1.0 + beta * (own_first(m + 1) + (own_last(m) - low * gamma)))
+            gamma = beta * cross(m + 1)
+            for q, value in enumerate((beta, beta * low, gamma)):
+                for ref in keep:
+                    ref[m, q] = value
+
+    def fluxes(jump, line, shape, put):
+        flux = jnp.zeros(shape, F32)
+        reduced = []
+        for m in range(others):
+            flux = line[m, 0] * jump(m) + line[m, 1] * flux
+            reduced.append(flux)
+        flux = jnp.zeros(shape, F32)
+        put(others, 1, flux)
+        put(0, 0, flux)
+        for m in reversed(range(others)):
+            flux = reduced[m] + line[m, 2] * flux
+            put(m, 1, flux)
+            put(m + 1, 0, flux)
+
+    for halo in halos:
+        halo.wait_recv()
     from_west, from_east = halo_in[0], halo_in[1]
     edges = []
     for t in range(4):
@@ -248,7 +298,36 @@
         p8 = p8 + edge_g8[y] * value
     msg_pe[0] = p1
     msg_pe[1] = p8
-    send(1, msg_pe, got_pe, e_ss.at[1], e_rs.at[1])
+    send_to_ends(msg_pe, got_pe, 1)
+
+    @pl.when(solver)
+    def _():
+        total(got_g.at[pl.ds(0, others)], g_ss, g_rs).wait_recv()
+
+        def part(q):
+            return lambda b: got_g[b, 2 * q : 2 * q + 2, :]
+
+        lines(
+            lambda m: jnp.minimum(part(4)(m), part(3)(m + 1)), part(0), part(1), part(2),
+            (2, LANES), [line_s.at[:, :, pl.ds(2 * f, 2)] for f in range(FIELDS)],
+        )
+        total(got_p.at[pl.ds(0, others)], p_ss, p_rs).wait_recv()
+
+        def put(b, end, flux):
+            msg_f[b, 4 * end : 4 * end + 4, :] = flux
+
+        fluxes(
+            lambda m: got_p[m + 1, 0:4, :] - got_p[m, 4:8, :], line_s, (4, LANES), put
+        )
+
+        @pl.loop(0, n_lat)
+        def _(k):
+            @pl.when(k != lat)
+            def _():
+                tile_to(msg_f, got_f, f_ss, f_rs, k).start()
+
+        got_f[lat] = msg_f[lat]
+
 
     for t in range(4):
         for g in range(COUNTS[t]):
@@ -278,101 +357,45 @@
         stacked = jnp.concatenate([high, root - high], axis=0)
         weights.append((stacked + roll(stacked, 32)).astype(BF16)[:, :64])
 
-    def total(ref, ss, rs):
-        return pltpu.make_async_remote_copy(
-            src_ref=ref, dst_ref=ref, send_sem=ss, recv_sem=rs,
-            device_id={"lat": lax.rem(lat + 1, n_lat)}, device_id_type=MESH,
-        )
-
-    others = pl.ds(0, n_lat - 1)
-
-    def lines(block, shape, keep):
-        gamma = jnp.zeros(shape, F32)
-        for m in range(n_lat - 1):
-            u = jnp.minimum(block(m, 4), block(m + 1, 3))
-            low = block(m, 2)
-            own = block(m + 1, 0) + (block(m, 1) - low * gamma)
-            beta = u / (1.0 + u * own)
-            gamma = beta * block(m + 1, 2)
-            for q, value in enumerate((beta, beta * low, gamma)):
-                keep[m, q] = value
-
-    def fluxes(jump, line, shape, put):
-        flux = jnp.zeros(shape, F32)
-        reduced = []
-        for m in range(n_lat - 1):
-            flux = line(m, 0) * jump(m) + line(m, 1) * flux
-            reduced.append(flux)
-        flux = jnp.zeros(shape, F32)
-        put(n_lat - 1, 1, flux)
-        put(0, 0, flux)
-        for m in reversed(range(n_lat - 1)):
-            flux = reduced[m] + line(m, 2) * flux
-            put(m, 1, flux)
-            put(m + 1, 0, flux)
-
-    for h in range(SOLVERS):
-
-        @pl.when(lat == h)
-        def _():
-            total(got_g.at[others], g_ss.at[h], g_rs.at[h]).wait_recv()
-            lines(lambda b, q: got_g[b, q], (HALF, LANES), line_s)
-            if h == 1:
-                total(got_ge.at[others], e_ss.at[0, h], e_rs.at[0, h]).wait_recv()
-                for e in range(2):
-                    lines(lambda b, q: got_ge[b, q], (4, LANES), line_e.at[:, :, pl.ds(4 * e, 4)])
-            total(got_p.at[others], p_ss.at[h], p_rs.at[h]).wait_recv()
-            for f in range(FIELDS):
-
-                def put(b, end, flux):
-                    msg_f[b, 2 * f + end] = flux
-
-                fluxes(
-                    lambda m: got_p[m + 1, 2 * f] - got_p[m, 2 * f + 1],
-                    lambda m, q: line_s[m, q], (HALF, LANES), put,
-                )
-
-            @pl.loop(1, n_lat)
-            def _(d):
-                of_solver(msg_f, got_f.at[h], h, lax.rem(lat + d, n_lat), f_ss, f_rs).start()
-
-            got_f[h] = msg_f[h]
-
-    for h in range(SOLVERS):
-
-        @pl.when(lat != h)
-        def _():
-            of_solver(msg_f, got_f.at[h], h, h, f_ss, f_rs).wait_recv()
-
-        flux_s[h, :, 0:HALF] = got_f[h]
-
-    @pl.when(lat == 1)
-    def _():
-        total(got_pe.at[others], e_ss.at[1, 1], e_rs.at[1, 1]).wait_recv()
+    @pl.when(lat == ENDS)
+    def _():
+        total(got_ge.at[pl.ds(0, others)], e_ss.at[0], e_rs.at[0]).wait_recv()
+        lines(
+            lambda m: jnp.minimum(got_ge[m, 4], got_ge[m + 1, 3]),
+            lambda b: got_ge[b, 0], lambda b: got_ge[b, 1], lambda b: got_ge[b, 2],
+            (4, LANES), [line_e.at[:, :, pl.ds(4 * f, 4)] for f in range(FIELDS)],
+        )
+        total(got_pe.at[pl.ds(0, others)], e_ss.at[1], e_rs.at[1]).wait_recv()
 
         def put(b, end, flux):
             msg_fe[b, end] = flux
 
-        fluxes(
-            lambda m: got_pe[m + 1, 0] - got_pe[m, 1],
-            lambda m, q: line_e[m, q], (ROWS, LANES), put,
-        )
+        fluxes(lambda m: got_pe[m + 1, 0] - got_pe[m, 1], line_e, (ROWS, LANES), put)
 
         @pl.loop(1, n_lat)
         def _(d):
-            of_solver(msg_fe, got_fe, 1, lax.rem(lat + d, n_lat), e_ss.at[2], e_rs.at[2]).start()
-
-        got_fe[...] = msg_fe[1]
-
-    @pl.when(lat != 1)
-    def _():
-        of_solver(msg_fe, got_fe, 1, 1, e_ss.at[2], e_rs.at[2]).wait_recv()
+            of_ends(lax.rem(lat + d, n_lat)).start()
+
+        got_fe[...] = msg_fe[ENDS]
+
+    @pl.when(solver)
+    def _():
+        total(got_f.at[pl.ds(0, HALF - 1)], f_ss, f_rs).wait_recv()
+
+    @pl.when(jnp.logical_not(solver))
+    def _():
+        total(got_f.at[pl.ds(0, HALF)], f_ss, f_rs).wait_recv()
+
+    @pl.when(lat != ENDS)
+    def _():
+        of_ends(ENDS).wait_recv()
 
     flux_e = roll(got_fe[...], -8)
     for f in range(FIELDS):
         for h in range(2):
             flux = []
             for end in range(2):
+                inside = got_f[:, 4 * end + 2 * f + h, :]
                 tiles = []
                 for a in range(2):
                     row = 4 * f + 2 * h + a
@@ -381,7 +404,7 @@
                         0, axis=1, stride=16, stride_axis=0,
                     )
                     tiles.append(
-                        jnp.where(edge, ends, flux_s[h, 2 * f + end, ROWS * a : ROWS * (a + 1)])
+                        jnp.where(edge, ends, inside[ROWS * a : ROWS * (a + 1)])
                     )
                 flux.append(jnp.concatenate(tiles, axis=0))
             for y in range(ROWS):
@@ -399,21 +422,26 @@
 
     for halo in halos:
         halo.wait_send()
-    for h in range(SOLVERS):
-
-        @pl.when(lat != h)
-        def _():
-            to_solver(msg_g.at[h], got_g, h, g_ss, g_rs).wait_send()
-            to_solver(msg_p.at[h], got_p, h, p_ss, p_rs).wait_send()
-            if h == 1:
-                to_solver(msg_ge, got_ge, h, e_ss.at[0], e_rs.at[0]).wait_send()
-                to_solver(msg_pe, got_pe, h, e_ss.at[1], e_rs.at[1]).wait_send()
-
-        @pl.when(lat == h)
-        def _():
-            total(msg_f.at[others], f_ss.at[h], f_rs.at[h]).wait_send()
-            if h == 1:
-                total(msg_fe.at[others], e_ss.at[2, h], e_rs.at[2, h]).wait_send()
+
+    @pl.when(lat != ENDS)
+    def _():
+        to_ends(msg_ge, got_ge, 0).wait_send()
+        to_ends(msg_pe, got_pe, 1).wait_send()
+
+    @pl.when(lat == ENDS)
+    def _():
+        total(msg_fe.at[pl.ds(0, others)], e_ss.at[2], e_rs.at[2]).wait_send()
+
+    @pl.when(solver)
+    def _():
+        total(msg_g.at[pl.ds(0, HALF - 1)], g_ss, g_rs).wait_send()
+        total(msg_p.at[pl.ds(0, HALF - 1)], p_ss, p_rs).wait_send()
+        total(msg_f.at[pl.ds(0, others)], f_ss, f_rs).wait_send()
+
+    @pl.when(jnp.logical_not(solver))
+    def _():
+        total(msg_g.at[pl.ds(0, HALF)], g_ss, g_rs).wait_send()
+        total(msg_p.at[pl.ds(0, HALF)], p_ss, p_rs).wait_send()
 
 
 def solution(mesh):
@@ -439,15 +467,14 @@
             (FIELDS,) + rows,
             (64, LANES), (64, LANES),
             (ROWS, ROWS, LANES), (ROWS, ROWS, LANES),
-            (SOLVERS, 5, HALF, LANES), (n_lat, 5, HALF, LANES),
-            (SOLVERS, 4, HALF, LANES), (n_lat, 4, HALF, LANES),
-            (n_lat, 4, HALF, LANES), (SOLVERS, 4, HALF, LANES),
+            (HALF, 10, LANES), (n_lat, 10, LANES),
+            (HALF, ROWS, LANES), (n_lat, ROWS, LANES),
+            (n_lat, ROWS, LANES), (16, ROWS, LANES),
             (5, 4, LANES), (n_lat, 5, 4, LANES),
             (2, ROWS, LANES), (n_lat, 2, ROWS, LANES),
             (n_lat, 2, ROWS, LANES), (2, ROWS, LANES),
-            (n_lat - 1, 3, HALF, LANES),
+            (n_lat - 1, 3, 4, LANES),
             (n_lat - 1, 3, ROWS, LANES),
-            (SOLVERS, 4, 16, LANES),
             (FIELDS, 32, LANES),
             ((FIELDS, 64, ROWS * LANES), BF16),
         ]
@@ -455,7 +482,7 @@
             pltpu.VMEM(*item) if isinstance(item[0], tuple) else pltpu.VMEM(item, F32)
             for item in scratch
         ]
-        sems = [(5,), (2,), (2,)] + [(SOLVERS,)] * 6 + [(3, SOLVERS)] * 2
+        sems = [(5,), (2,), (2,)] + [()] * 6 + [(3,)] * 2
         made = pl.pallas_call(
             functools.partial(kernel, n_lon, n_lat),
             out_shape=pltpu.VMEM((FIELDS, LEV * ROWS, LANES), F32),

time: 32 us -> 26.8 us (0.84)
  Pallas kernels: 31.1 us -> 26 us
    pallas_call x1, Pallas kernels: 31.1 us -> 26 us  [per_device(): pl.pallas_call(functools.partial(kernel, n_lon, n_lat), out_shape=pltpu.V...]
where the time goes in v3:
time: 26.8 us; the launch traced here: 26.6 us
  Pallas kernels  26 us (97%)
  local copies, waits for them, and re-layouts  0.68 us (3%)
    pallas_call x1, Pallas kernels, per_device(): pl.pallas_call(functools.partial(kernel, n_lon, n_lat), out_shape=pltpu.V...  26 us
    unnamed x1, local copies, waits for them, and re-layouts  0.68 us

profile of v3, /device:TPU:1, one launch (start us, length us, event | category | flops | bytes accessed | tf_op | source)
XLA Modules:
  0.0 26.6 jit_solution(631369522123592463)
XLA Ops:
  0.0 26.0 %shard_map.55 = f32[2,200,128]{2,1,0:T(8,128)S(1)} custom-call(f32[2,25,8,128]{3,2,1,0:T(8,128)} %tr_h.1, s32[25,8,128]{2,1,0:T(8,128)} %mk_h.1, bf16[25,8,128]{2,1,0:T(8,128)(2,1)} %kl_h.1, bf16[25,8,128]{2,1,0:T(8,128)(2,1)} %kt_h.1, f32[25,2,25]{2,1,0:T(2,128)} %bitcast.3), custom_call_target="tpu_custom_call" | custom-call | tf_op jit(solution)/shard_map/pallas_call | solution.py:486
  26.0 0.7 %copy.7 = f32[2,25,8,128]{3,2,1,0:T(8,128)} copy(f32[2,25,8,128]{3,2,1,0:T(8,128)S(1)} %bitcast.2) | data formatting | bytes 409600

commit v4 on v3

--- a/solution.py
+++ b/solution.py
@@ -13,7 +13,7 @@
 ROWS = 8
 LANES = 128
 HALF = 13
-ENDS = 1
+ENDS = 2
 PAD = HALF + 16
 STARTS = (0, 8, 13, 21)
 COUNTS = (8, 5, 8, 4)
@@ -75,7 +75,7 @@
     msg_g, got_g, msg_p, got_p, msg_f, got_f,
     msg_ge, got_ge, msg_pe, got_pe, msg_fe, got_fe,
     line_s, line_e, vpad, x_s,
-    in_sem, halo_ss, halo_rs, g_ss, g_rs, p_ss, p_rs, f_ss, f_rs, e_ss, e_rs,
+    in_sem, halo_ss, halo_rs, g_ss, g_rs, p_ss, p_rs, f_ss, f_rs, fe_ss, fe_rs, e_ss, e_rs, here,
 ):
     lon, lat = lax.axis_index("lon"), lax.axis_index("lat")
     east, west = lax.rem(lon + 1, n_lon), lax.rem(lon + n_lon - 1, n_lon)
@@ -91,8 +91,7 @@
         load.start()
 
     barrier = pltpu.get_barrier_semaphore()
-    for side in (east, west):
-        pl.semaphore_signal(barrier, inc=1, device_id={"lon": side}, device_id_type=MESH)
+    pl.semaphore_signal(barrier, inc=1, device_id={"lon": west}, device_id_type=MESH)
 
     @pl.when(solver)
     def _():
@@ -147,14 +146,14 @@
 
     @pl.when(solver)
     def _():
+        pl.semaphore_wait(barrier, HALF)
+
+    @pl.when(jnp.logical_not(solver))
+    def _():
         pl.semaphore_wait(barrier, HALF + 1)
 
-    @pl.when(jnp.logical_not(solver))
-    def _():
-        pl.semaphore_wait(barrier, HALF + 2)
-
-    for halo in halos:
-        halo.start()
+    halos[0].start()
+    pl.semaphore_signal(here, inc=1, device_id={"lon": east}, device_id_type=MESH)
 
     def tile_to(msg, got, ss, rs, k):
         return pltpu.make_async_remote_copy(
@@ -181,26 +180,28 @@
             device_id={"lat": lax.rem(lat + 1, n_lat)}, device_id_type=MESH,
         )
 
-    def to_ends(msg, got, i):
+    def to_ends(msg, got, kind, k):
         return pltpu.make_async_remote_copy(
-            src_ref=msg, dst_ref=got.at[lat], send_sem=e_ss.at[i], recv_sem=e_rs.at[i],
-            device_id={"lat": ENDS}, device_id_type=MESH,
+            src_ref=msg, dst_ref=got.at[lat], send_sem=e_ss.at[kind, k], recv_sem=e_rs.at[kind],
+            device_id={"lat": k}, device_id_type=MESH,
         )
 
     def of_ends(k):
         return pltpu.make_async_remote_copy(
-            src_ref=msg_fe.at[k], dst_ref=got_fe, send_sem=e_ss.at[2], recv_sem=e_rs.at[2],
+            src_ref=msg_fe.at[k], dst_ref=got_fe, send_sem=fe_ss, recv_sem=fe_rs,
             device_id={"lat": k}, device_id_type=MESH,
         )
 
-    def send_to_ends(msg, got, i):
-        @pl.when(lat != ENDS)
-        def _():
-            to_ends(msg, got, i).start()
-
-        @pl.when(lat == ENDS)
-        def _():
-            got[ENDS] = msg[...]
+    def send_to_ends(msg, got, kind):
+        for k in range(ENDS):
+
+            @pl.when(lat != k)
+            def _():
+                to_ends(msg, got, kind, k).start()
+
+            @pl.when(lat == k)
+            def _():
+                got[k] = msg[...]
 
     loads[3].wait()
     lat_s[pl.ds(0, LEV * ROWS), :] = kt[...].astype(F32).reshape(LEV * ROWS, LANES) * ocean_s[...]
@@ -277,6 +278,8 @@
             put(m, 1, flux)
             put(m + 1, 0, flux)
 
+    pl.semaphore_wait(here, 1)
+    halos[1].start()
     for halo in halos:
         halo.wait_recv()
     from_west, from_east = halo_in[0], halo_in[1]
@@ -357,26 +360,27 @@
         stacked = jnp.concatenate([high, root - high], axis=0)
         weights.append((stacked + roll(stacked, 32)).astype(BF16)[:, :64])
 
-    @pl.when(lat == ENDS)
-    def _():
-        total(got_ge.at[pl.ds(0, others)], e_ss.at[0], e_rs.at[0]).wait_recv()
+    @pl.when(lat < ENDS)
+    def _():
+        total(got_ge.at[pl.ds(0, others)], e_ss.at[0, 0], e_rs.at[0]).wait_recv()
         lines(
             lambda m: jnp.minimum(got_ge[m, 4], got_ge[m + 1, 3]),
             lambda b: got_ge[b, 0], lambda b: got_ge[b, 1], lambda b: got_ge[b, 2],
             (4, LANES), [line_e.at[:, :, pl.ds(4 * f, 4)] for f in range(FIELDS)],
         )
-        total(got_pe.at[pl.ds(0, others)], e_ss.at[1], e_rs.at[1]).wait_recv()
+        total(got_pe.at[pl.ds(0, others)], e_ss.at[1, 0], e_rs.at[1]).wait_recv()
 
         def put(b, end, flux):
             msg_fe[b, end] = flux
 
         fluxes(lambda m: got_pe[m + 1, 0] - got_pe[m, 1], line_e, (ROWS, LANES), put)
-
-        @pl.loop(1, n_lat)
-        def _(d):
-            of_ends(lax.rem(lat + d, n_lat)).start()
-
-        got_fe[...] = msg_fe[ENDS]
+        got_fe[...] = msg_fe[lat]
+
+    @pl.when(lat == 0)
+    def _():
+        @pl.loop(ENDS, n_lat)
+        def _(k):
+            of_ends(k).start()
 
     @pl.when(solver)
     def _():
@@ -386,9 +390,9 @@
     def _():
         total(got_f.at[pl.ds(0, HALF)], f_ss, f_rs).wait_recv()
 
-    @pl.when(lat != ENDS)
-    def _():
-        of_ends(ENDS).wait_recv()
+    @pl.when(lat >= ENDS)
+    def _():
+        of_ends(lat).wait_recv()
 
     flux_e = roll(got_fe[...], -8)
     for f in range(FIELDS):
@@ -423,14 +427,16 @@
     for halo in halos:
         halo.wait_send()
 
-    @pl.when(lat != ENDS)
-    def _():
-        to_ends(msg_ge, got_ge, 0).wait_send()
-        to_ends(msg_pe, got_pe, 1).wait_send()
-
-    @pl.when(lat == ENDS)
-    def _():
-        total(msg_fe.at[pl.ds(0, others)], e_ss.at[2], e_rs.at[2]).wait_send()
+    for k in range(ENDS):
+
+        @pl.when(lat != k)
+        def _():
+            to_ends(msg_ge, got_ge, 0, k).wait_send()
+            to_ends(msg_pe, got_pe, 1, k).wait_send()
+
+    @pl.when(lat == 0)
+    def _():
+        total(msg_fe.at[pl.ds(0, n_lat - ENDS)], fe_ss, fe_rs).wait_send()
 
     @pl.when(solver)
     def _():
@@ -482,13 +488,15 @@
             pltpu.VMEM(*item) if isinstance(item[0], tuple) else pltpu.VMEM(item, F32)
             for item in scratch
         ]
-        sems = [(5,), (2,), (2,)] + [()] * 6 + [(3,)] * 2
+        sems = [(5,), (2,), (2,)] + [()] * 8 + [(2, ENDS), (2,)]
         made = pl.pallas_call(
             functools.partial(kernel, n_lon, n_lat),
             out_shape=pltpu.VMEM((FIELDS, LEV * ROWS, LANES), F32),
             in_specs=[pl.BlockSpec(memory_space=pltpu.HBM)] * 5,
             out_specs=pl.BlockSpec(memory_space=pltpu.VMEM),
-            scratch_shapes=scratch + [pltpu.SemaphoreType.DMA(shape) for shape in sems],
+            scratch_shapes=scratch
+            + [pltpu.SemaphoreType.DMA(shape) for shape in sems]
+            + [pltpu.SemaphoreType.REGULAR],
             compiler_params=pltpu.CompilerParams(
                 collective_id=0, has_side_effects=True, vmem_limit_bytes=60 * 1024 * 1024
             ),

time: 26.8 us -> 24.9 us (0.929)
  Pallas kernels: 26 us -> 24.1 us
    pallas_call x1, Pallas kernels: 26 us -> 24.1 us  [per_device(): pl.pallas_call(functools.partial(kernel, n_lon, n_lat), out_shape=pltpu.V...]
where the time goes in v4:
time: 24.9 us; the launch traced here: 24.8 us
  Pallas kernels  24.1 us (97%)
  local copies, waits for them, and re-layouts  0.68 us (3%)
    pallas_call x1, Pallas kernels, per_device(): pl.pallas_call(functools.partial(kernel, n_lon, n_lat), out_shape=pltpu.V...  24.1 us
    unnamed x1, local copies, waits for them, and re-layouts  0.68 us

profile of v4, /device:TPU:1, one launch (start us, length us, event | category | flops | bytes accessed | tf_op | source)
XLA Modules:
  0.0 24.8 jit_solution(4296786159551353887)
XLA Ops:
  0.0 24.1 %shard_map.55 = f32[2,200,128]{2,1,0:T(8,128)S(1)} custom-call(f32[2,25,8,128]{3,2,1,0:T(8,128)} %tr_h.1, s32[25,8,128]{2,1,0:T(8,128)} %mk_h.1, bf16[25,8,128]{2,1,0:T(8,128)(2,1)} %kl_h.1, bf16[25,8,128]{2,1,0:T(8,128)(2,1)} %kt_h.1, f32[25,2,25]{2,1,0:T(2,128)} %bitcast.3), custom_call_target="tpu_custom_call" | custom-call | tf_op jit(solution)/shard_map/pallas_call | solution.py:492
  24.1 0.7 %copy.7 = f32[2,25,8,128]{3,2,1,0:T(8,128)} copy(f32[2,25,8,128]{3,2,1,0:T(8,128)S(1)} %bitcast.2) | data formatting | bytes 409600

commit v5 on v4

--- a/solution.py
+++ b/solution.py
@@ -13,7 +13,10 @@
 ROWS = 8
 LANES = 128
 HALF = 13
-ENDS = 2
+FEW = 7
+TILES = 2 * FEW
+RING, TOP = 8, 4
+ENDS = 3
 PAD = HALF + 16
 STARTS = (0, 8, 13, 21)
 COUNTS = (8, 5, 8, 4)
@@ -72,14 +75,22 @@
     tr, mk, kl, kt, vr,
     lon_s, halo_out, halo_in, lat_s, diff_s, ocean_s,
     ratio_s, ipiv_s, g1_s, g8_s, part_s, edge_c, edge_s, edge_g1, edge_g8,
-    msg_g, got_g, msg_p, got_p, msg_f, got_f,
+    two_g, two_p, joint_s, msg_g, got_g, msg_p, got_p, msg_f, got_f, flux_s,
     msg_ge, got_ge, msg_pe, got_pe, msg_fe, got_fe,
     line_s, line_e, vpad, x_s,
-    in_sem, halo_ss, halo_rs, g_ss, g_rs, p_ss, p_rs, f_ss, f_rs, fe_ss, fe_rs, e_ss, e_rs, here,
+    in_sem, halo_ss, halo_rs, g_ss, g_rs, p_ss, p_rs, f_ss, f_rs, fe_ss, fe_rs, e_ss, e_rs, two_ss, two_rs, here,
 ):
     lon, lat = lax.axis_index("lon"), lax.axis_index("lat")
     east, west = lax.rem(lon + 1, n_lon), lax.rem(lon + n_lon - 1, n_lon)
-    solver = lat < HALF
+    last = lon == n_lon - 1
+    hosts = jnp.where(last, FEW, TILES)
+    solver = lat < hosts
+    core, mate = lat & 1, lat ^ 1
+    own = (
+        (jnp.logical_not(solver), 0),
+        (solver & jnp.logical_not(last), 1),
+        (solver & last, 2),
+    )
 
     loads = [
         pltpu.make_async_copy(src, dst, in_sem.at[i])
@@ -90,8 +101,15 @@
     for load in loads:
         load.start()
 
+    at = lax.rem(lon, RING)
+    early = (at >= TOP, (at >= 1) & (at <= TOP))
+    late = (at < TOP, (at > TOP) | (at == 0))
     barrier = pltpu.get_barrier_semaphore()
-    pl.semaphore_signal(barrier, inc=1, device_id={"lon": west}, device_id_type=MESH)
+    for side, is_late in zip((east, west), late):
+
+        @pl.when(is_late)
+        def _():
+            pl.semaphore_signal(barrier, inc=1, device_id={"lon": side}, device_id_type=MESH)
 
     @pl.when(solver)
     def _():
@@ -101,12 +119,19 @@
                 barrier, inc=1, device_id={"lat": lax.rem(lat + d, n_lat)}, device_id_type=MESH
             )
 
+    @pl.when(jnp.logical_not(solver))
+    def _():
+        pl.semaphore_signal(barrier, inc=1, device_id={"lat": mate}, device_id_type=MESH)
+
+    others, chips = n_lat - 1, n_lat // 2
     lane = lax.broadcasted_iota(jnp.int32, (ROWS, LANES), 1)
     slot = (lane >> 2) & 3
     group = lane >> 4
     edge = (lane < 4) | (lane >= LANES - 4)
 
-    got_f[HALF:16] = jnp.zeros((16 - HALF, ROWS, LANES), F32)
+    flux_s[TILES:16] = jnp.zeros((16 - TILES, ROWS, LANES), F32)
+    two_g[core, HALF:TILES] = jnp.zeros((TILES - HALF, 10, LANES), F32)
+    two_p[core, HALF:TILES] = jnp.zeros((TILES - HALF, ROWS, LANES), F32)
     vpad[...] = jnp.zeros(vpad.shape, F32)
     spare = pl.ds(LEV * ROWS, (PAD - LEV) * ROWS)
     lat_s[spare, :] = jnp.zeros(((PAD - LEV) * ROWS, LANES), F32)
@@ -144,35 +169,50 @@
         for i, side in enumerate((east, west))
     ]
 
-    @pl.when(solver)
-    def _():
-        pl.semaphore_wait(barrier, HALF)
-
-    @pl.when(jnp.logical_not(solver))
-    def _():
-        pl.semaphore_wait(barrier, HALF + 1)
-
-    halos[0].start()
-    pl.semaphore_signal(here, inc=1, device_id={"lon": east}, device_id_type=MESH)
-
-    def tile_to(msg, got, ss, rs, k):
+    count = hosts - solver.astype(jnp.int32) + (mate >= hosts).astype(jnp.int32)
+    for is_early in early:
+        count = count + is_early.astype(jnp.int32)
+    pl.semaphore_wait(barrier, count)
+    for i in range(2):
+
+        @pl.when(early[i])
+        def _():
+            halos[i].start()
+            pl.semaphore_signal(
+                here.at[1 - i], inc=1, device_id={"lon": (east, west)[i]}, device_id_type=MESH
+            )
+
+    def send_to_hosts(msg, got, ss, rs):
+        for j in range(FEW):
+            tile = 2 * j + core
+            host = jnp.where(last, j, tile)
+            place = jnp.where(last, core, 0) * chips + (lat >> 1)
+
+            @pl.when(lat != host)
+            def _():
+                pltpu.make_async_remote_copy(
+                    src_ref=msg.at[tile], dst_ref=got.at[place],
+                    send_sem=ss, recv_sem=rs, device_id={"lat": host}, device_id_type=MESH,
+                ).start()
+
+            @pl.when(lat == host)
+            def _():
+                got[place] = msg[tile]
+
+    def flux_tile(place):
+        return jnp.where(last, 2 * lat + place, lat)
+
+    def flux_to(place, k):
         return pltpu.make_async_remote_copy(
-            src_ref=msg.at[k], dst_ref=got.at[lat],
-            send_sem=ss, recv_sem=rs, device_id={"lat": k}, device_id_type=MESH,
-        )
-
-    def send_to_solvers(msg, got, ss, rs):
-        @pl.loop(1, n_lat)
-        def _(d):
-            k = lax.rem(lat + d, n_lat)
-
-            @pl.when(k < HALF)
-            def _():
-                tile_to(msg, got, ss, rs, k).start()
-
-        @pl.when(solver)
-        def _():
-            got[lat] = msg[lat]
+            src_ref=msg_f.at[place, k], dst_ref=got_f.at[flux_tile(place)],
+            send_sem=f_ss, recv_sem=f_rs, device_id={"lat": k}, device_id_type=MESH,
+        )
+
+    def to_mate(ref, ss, rs):
+        return pltpu.make_async_remote_copy(
+            src_ref=ref.at[core], dst_ref=ref.at[core],
+            send_sem=ss, recv_sem=rs, device_id={"lat": mate}, device_id_type=MESH,
+        )
 
     def total(ref, ss, rs):
         return pltpu.make_async_remote_copy(
@@ -193,7 +233,7 @@
         )
 
     def send_to_ends(msg, got, kind):
-        for k in range(ENDS):
+        for k in (1, 0, 2):
 
             @pl.when(lat != k)
             def _():
@@ -213,8 +253,8 @@
             ratio_s[y] = ratio[y]
     for h in range(2):
         for q, value in enumerate((g1[0], g8[-1], g8[0], coef[0], coef[-1])):
-            msg_g[:, 2 * q + h, :] = value[h, :HALF]
-    send_to_solvers(msg_g, got_g, g_ss, g_rs)
+            two_g[core, 0:HALF, 2 * q + h, :] = value[h, :HALF]
+    to_mate(two_g, two_ss.at[0], two_rs.at[0]).start()
     for t in range(4):
         tile = roll(lat_s[pl.ds(STARTS[t] * ROWS, ROWS), :], 8)
         for g in range(1, COUNTS[t]):
@@ -229,7 +269,6 @@
         edge_g1[y], edge_g8[y] = g1[y], g8[y]
     for q, value in enumerate((g1[0], g8[-1], g8[0], coef[0], coef[-1])):
         msg_ge[q] = value[0:4]
-    send_to_ends(msg_ge, got_ge, 0)
 
     for t in range(4):
         n = COUNTS[t]
@@ -247,15 +286,40 @@
             p1 = p1 + g1_s[y] * value
             p8 = p8 + g8_s[y] * value
         for h in range(2):
-            msg_p[:, 2 * f + h, :] = p1[h, :HALF]
-            msg_p[:, 4 + 2 * f + h, :] = p8[h, :HALF]
-    send_to_solvers(msg_p, got_p, p_ss, p_rs)
-
-    others = n_lat - 1
-
-    def lines(face, own_first, own_last, cross, shape, keep):
+            two_p[core, 0:HALF, 2 * f + h, :] = p1[h, :HALF]
+            two_p[core, 0:HALF, 4 + 2 * f + h, :] = p8[h, :HALF]
+
+    to_mate(two_p, two_ss.at[1], two_rs.at[1]).start()
+
+    def lower(q):
+        return two_g[0, :, 2 * q : 2 * q + 2, :]
+
+    def upper(q):
+        return two_g[1, :, 2 * q : 2 * q + 2, :]
+
+    to_mate(two_g, two_ss.at[0], two_rs.at[0]).wait_recv()
+    face = jnp.minimum(lower(4), upper(3))
+    weight = face / (1.0 + face * (lower(1) + upper(0)))
+    low_g, up_g = weight * lower(2), weight * upper(2)
+    for q, value in enumerate(
+        (lower(0) - low_g * lower(2), upper(1) - up_g * upper(2), low_g * upper(2), lower(3), upper(4))
+    ):
+        msg_g[:, 2 * q : 2 * q + 2, :] = value
+    for f in range(FIELDS):
+        for q, value in enumerate((weight, low_g, up_g)):
+            joint_s[q, :, 2 * f : 2 * f + 2, :] = value
+    send_to_hosts(msg_g, got_g, g_ss, g_rs)
+    to_mate(two_p, two_ss.at[1], two_rs.at[1]).wait_recv()
+    jump = two_p[1, :, 0:4, :] - two_p[0, :, 4:8, :]
+    msg_p[:, 0:4, :] = two_p[0, :, 0:4, :] + joint_s[1] * jump
+    msg_p[:, 4:8, :] = two_p[1, :, 4:8, :] - joint_s[2] * jump
+    send_to_hosts(msg_p, got_p, p_ss, p_rs)
+    send_to_ends(msg_ge, got_ge, 0)
+
+
+    def lines(count, face, own_first, own_last, cross, shape, keep):
         gamma = jnp.zeros(shape, F32)
-        for m in range(others):
+        for m in range(count):
             low = cross(m)
             beta = face(m)
             beta = beta / (1.0 + beta * (own_first(m + 1) + (own_last(m) - low * gamma)))
@@ -264,22 +328,27 @@
                 for ref in keep:
                     ref[m, q] = value
 
-    def fluxes(jump, line, shape, put):
+    def fluxes(count, jump, line, shape, put):
         flux = jnp.zeros(shape, F32)
         reduced = []
-        for m in range(others):
+        for m in range(count):
             flux = line[m, 0] * jump(m) + line[m, 1] * flux
             reduced.append(flux)
         flux = jnp.zeros(shape, F32)
-        put(others, 1, flux)
+        put(count, 1, flux)
         put(0, 0, flux)
-        for m in reversed(range(others)):
+        for m in reversed(range(count)):
             flux = reduced[m] + line[m, 2] * flux
             put(m, 1, flux)
             put(m + 1, 0, flux)
 
-    pl.semaphore_wait(here, 1)
-    halos[1].start()
+    for i in range(2):
+
+        @pl.when(late[i])
+        def _():
+            pl.semaphore_wait(here.at[i], 1)
+            halos[i].start()
+
     for halo in halos:
         halo.wait_recv()
     from_west, from_east = halo_in[0], halo_in[1]
@@ -299,38 +368,49 @@
         value = by_row(edge_s, y)
         p1 = p1 + edge_g1[y] * value
         p8 = p8 + edge_g8[y] * value
-    msg_pe[0] = p1
-    msg_pe[1] = p8
+    msg_pe[...] = jnp.where((slot == 1) | (slot == 2), p1, roll(p8, 8))
     send_to_ends(msg_pe, got_pe, 1)
 
-    @pl.when(solver)
-    def _():
-        total(got_g.at[pl.ds(0, others)], g_ss, g_rs).wait_recv()
+    def solve(places):
+        def held(ref, b, rows):
+            return jnp.stack([ref[chips * place + b, rows, :] for place in range(places)])
 
         def part(q):
-            return lambda b: got_g[b, 2 * q : 2 * q + 2, :]
-
+            return lambda b: held(got_g, b, slice(2 * q, 2 * q + 2))
+
+        count = chips * places - 1
+        total(got_g.at[pl.ds(0, count)], g_ss, g_rs).wait_recv()
         lines(
-            lambda m: jnp.minimum(part(4)(m), part(3)(m + 1)), part(0), part(1), part(2),
-            (2, LANES), [line_s.at[:, :, pl.ds(2 * f, 2)] for f in range(FIELDS)],
-        )
-        total(got_p.at[pl.ds(0, others)], p_ss, p_rs).wait_recv()
+            chips - 1, lambda m: jnp.minimum(part(4)(m), part(3)(m + 1)),
+            part(0), part(1), part(2), (places, 2, LANES),
+            [line_s.at[:, :, pl.ds(0, places), pl.ds(2 * f, 2)] for f in range(FIELDS)],
+        )
+        total(got_p.at[pl.ds(0, count)], p_ss, p_rs).wait_recv()
 
         def put(b, end, flux):
-            msg_f[b, 4 * end : 4 * end + 4, :] = flux
+            for c in range(2):
+                msg_f[0:places, 2 * b + c, 4 * end : 4 * end + 4, :] = flux
 
         fluxes(
-            lambda m: got_p[m + 1, 0:4, :] - got_p[m, 4:8, :], line_s, (4, LANES), put
+            chips - 1, lambda m: held(got_p, m + 1, slice(0, 4)) - held(got_p, m, slice(4, 8)),
+            line_s.at[:, :, pl.ds(0, places)], (places, 4, LANES), put,
         )
 
         @pl.loop(0, n_lat)
         def _(k):
             @pl.when(k != lat)
             def _():
-                tile_to(msg_f, got_f, f_ss, f_rs, k).start()
-
-        got_f[lat] = msg_f[lat]
-
+                for place in range(places):
+                    flux_to(place, k).start()
+
+        for place in range(places):
+            got_f[flux_tile(place)] = msg_f[place, lat]
+
+    for holds, places in own[1:]:
+
+        @pl.when(holds)
+        def _():
+            solve(places)
 
     for t in range(4):
         for g in range(COUNTS[t]):
@@ -364,7 +444,7 @@
     def _():
         total(got_ge.at[pl.ds(0, others)], e_ss.at[0, 0], e_rs.at[0]).wait_recv()
         lines(
-            lambda m: jnp.minimum(got_ge[m, 4], got_ge[m + 1, 3]),
+            others, lambda m: jnp.minimum(got_ge[m, 4], got_ge[m + 1, 3]),
             lambda b: got_ge[b, 0], lambda b: got_ge[b, 1], lambda b: got_ge[b, 2],
             (4, LANES), [line_e.at[:, :, pl.ds(4 * f, 4)] for f in range(FIELDS)],
         )
@@ -373,22 +453,28 @@
         def put(b, end, flux):
             msg_fe[b, end] = flux
 
-        fluxes(lambda m: got_pe[m + 1, 0] - got_pe[m, 1], line_e, (ROWS, LANES), put)
+        jumps = [got_pe[m + 1] - roll(got_pe[m], -8) for m in range(others)]
+        fluxes(others, lambda m: jumps[m], line_e, (ROWS, LANES), put)
         got_fe[...] = msg_fe[lat]
 
-    @pl.when(lat == 0)
+    @pl.when(lat == ENDS - 1)
     def _():
         @pl.loop(ENDS, n_lat)
         def _(k):
             of_ends(k).start()
 
-    @pl.when(solver)
-    def _():
-        total(got_f.at[pl.ds(0, HALF - 1)], f_ss, f_rs).wait_recv()
-
-    @pl.when(jnp.logical_not(solver))
-    def _():
-        total(got_f.at[pl.ds(0, HALF)], f_ss, f_rs).wait_recv()
+    for holds, places in own:
+
+        @pl.when(holds)
+        def _():
+            total(got_f.at[pl.ds(0, TILES - places)], f_ss, f_rs).wait_recv()
+
+    low, up = got_f[0:TILES, 0:4, :], got_f[0:TILES, 4:8, :]
+    between = (
+        joint_s[0] * (two_p[1, :, 0:4, :] - two_p[0, :, 4:8, :]) + joint_s[1] * low + joint_s[2] * up
+    )
+    flux_s[0:TILES, 0:4, :] = jnp.where(core == 0, low, between)
+    flux_s[0:TILES, 4:8, :] = jnp.where(core == 0, between, up)
 
     @pl.when(lat >= ENDS)
     def _():
@@ -399,7 +485,7 @@
         for h in range(2):
             flux = []
             for end in range(2):
-                inside = got_f[:, 4 * end + 2 * f + h, :]
+                inside = flux_s[:, 4 * end + 2 * f + h, :]
                 tiles = []
                 for a in range(2):
                     row = 4 * f + 2 * h + a
@@ -426,6 +512,8 @@
 
     for halo in halos:
         halo.wait_send()
+    to_mate(two_g, two_ss.at[0], two_rs.at[0]).wait_send()
+    to_mate(two_p, two_ss.at[1], two_rs.at[1]).wait_send()
 
     for k in range(ENDS):
 
@@ -434,20 +522,18 @@
             to_ends(msg_ge, got_ge, 0, k).wait_send()
             to_ends(msg_pe, got_pe, 1, k).wait_send()
 
-    @pl.when(lat == 0)
+    @pl.when(lat == ENDS - 1)
     def _():
         total(msg_fe.at[pl.ds(0, n_lat - ENDS)], fe_ss, fe_rs).wait_send()
 
-    @pl.when(solver)
-    def _():
-        total(msg_g.at[pl.ds(0, HALF - 1)], g_ss, g_rs).wait_send()
-        total(msg_p.at[pl.ds(0, HALF - 1)], p_ss, p_rs).wait_send()
-        total(msg_f.at[pl.ds(0, others)], f_ss, f_rs).wait_send()
-
-    @pl.when(jnp.logical_not(solver))
-    def _():
-        total(msg_g.at[pl.ds(0, HALF)], g_ss, g_rs).wait_send()
-        total(msg_p.at[pl.ds(0, HALF)], p_ss, p_rs).wait_send()
+    for holds, places in own:
+
+        @pl.when(holds)
+        def _():
+            total(msg_g.at[pl.ds(0, FEW - min(places, 1))], g_ss, g_rs).wait_send()
+            total(msg_p.at[pl.ds(0, FEW - min(places, 1))], p_ss, p_rs).wait_send()
+            if places:
+                total(msg_f.at[pl.ds(0, places), pl.ds(0, others)], f_ss, f_rs).wait_send()
 
 
 def solution(mesh):
@@ -473,13 +559,14 @@
             (FIELDS,) + rows,
             (64, LANES), (64, LANES),
             (ROWS, ROWS, LANES), (ROWS, ROWS, LANES),
-            (HALF, 10, LANES), (n_lat, 10, LANES),
-            (HALF, ROWS, LANES), (n_lat, ROWS, LANES),
-            (n_lat, ROWS, LANES), (16, ROWS, LANES),
+            (2, TILES, 10, LANES), (2, TILES, ROWS, LANES), (3, TILES, 4, LANES),
+            (TILES, 10, LANES), (n_lat, 10, LANES),
+            (TILES, ROWS, LANES), (n_lat, ROWS, LANES),
+            (2, n_lat, ROWS, LANES), (TILES, ROWS, LANES), (16, ROWS, LANES),
             (5, 4, LANES), (n_lat, 5, 4, LANES),
-            (2, ROWS, LANES), (n_lat, 2, ROWS, LANES),
+            (ROWS, LANES), (n_lat, ROWS, LANES),
             (n_lat, 2, ROWS, LANES), (2, ROWS, LANES),
-            (n_lat - 1, 3, 4, LANES),
+            (n_lat // 2 - 1, 3, 2, 4, LANES),
             (n_lat - 1, 3, ROWS, LANES),
             (FIELDS, 32, LANES),
             ((FIELDS, 64, ROWS * LANES), BF16),
@@ -488,7 +575,7 @@
             pltpu.VMEM(*item) if isinstance(item[0], tuple) else pltpu.VMEM(item, F32)
             for item in scratch
         ]
-        sems = [(5,), (2,), (2,)] + [()] * 8 + [(2, ENDS), (2,)]
+        sems = [(5,), (2,), (2,)] + [()] * 8 + [(2, ENDS), (2,), (2,), (2,)]
         made = pl.pallas_call(
             functools.partial(kernel, n_lon, n_lat),
             out_shape=pltpu.VMEM((FIELDS, LEV * ROWS, LANES), F32),
@@ -496,7 +583,7 @@
             out_specs=pl.BlockSpec(memory_space=pltpu.VMEM),
             scratch_shapes=scratch
             + [pltpu.SemaphoreType.DMA(shape) for shape in sems]
-            + [pltpu.SemaphoreType.REGULAR],
+            + [pltpu.SemaphoreType.REGULAR((2,))],
             compiler_params=pltpu.CompilerParams(
                 collective_id=0, has_side_effects=True, vmem_limit_bytes=60 * 1024 * 1024
             ),

time: 24.9 us -> 24.1 us (0.968)
  Pallas kernels: 24.1 us -> 23.3 us
    pallas_call x1, Pallas kernels: 24.1 us -> 23.3 us  [per_device(): pl.pallas_call(functools.partial(kernel, n_lon, n_lat), out_shape=pltpu.V...]
where the time goes in v5:
time: 24.1 us; the launch traced here: 24 us
  Pallas kernels  23.3 us (97%)
  local copies, waits for them, and re-layouts  0.68 us (3%)
    pallas_call x1, Pallas kernels, per_device(): pl.pallas_call(functools.partial(kernel, n_lon, n_lat), out_shape=pltpu.V...  23.3 us
    unnamed x1, local copies, waits for them, and re-layouts  0.68 us

profile of v5, /device:TPU:1, one launch (start us, length us, event | category | flops | bytes accessed | tf_op | source)
XLA Modules:
  0.0 24.0 jit_solution(3965203916540019707)
XLA Ops:
  0.0 23.3 %shard_map.55 = f32[2,200,128]{2,1,0:T(8,128)S(1)} custom-call(f32[2,25,8,128]{3,2,1,0:T(8,128)} %tr_h.1, s32[25,8,128]{2,1,0:T(8,128)} %mk_h.1, bf16[25,8,128]{2,1,0:T(8,128)(2,1)} %kl_h.1, bf16[25,8,128]{2,1,0:T(8,128)(2,1)} %kt_h.1, f32[25,2,25]{2,1,0:T(2,128)} %bitcast.3), custom_call_target="tpu_custom_call" | custom-call | tf_op jit(solution)/shard_map/pallas_call | solution.py:579
  23.3 0.7 %copy.7 = f32[2,25,8,128]{3,2,1,0:T(8,128)} copy(f32[2,25,8,128]{3,2,1,0:T(8,128)S(1)} %bitcast.2) | data formatting | bytes 409600

commit v6 on v5

--- a/solution.py
+++ b/solution.py
@@ -95,11 +95,14 @@
     loads = [
         pltpu.make_async_copy(src, dst, in_sem.at[i])
         for i, (src, dst) in enumerate(
-            ((mk_h, mk), (kl_h, kl), (tr_h, tr), (kt_h, kt), (vr_h, vr))
+            (
+                (mk_h, mk), (kl_h, kl), (tr_h.at[0], tr.at[0]), (kt_h, kt), (vr_h, vr),
+                (tr_h.at[1], tr.at[1]),
+            )
         )
     ]
-    for load in loads:
-        load.start()
+    for i in (2, 5, 0, 1, 3, 4):
+        loads[i].start()
 
     at = lax.rem(lon, RING)
     early = (at >= TOP, (at >= 1) & (at <= TOP))
@@ -141,6 +144,7 @@
     loads[0].wait()
     loads[1].wait()
     loads[2].wait()
+    loads[5].wait()
     packed = []
     for t in range(4):
         n = COUNTS[t]
@@ -575,7 +579,7 @@
             pltpu.VMEM(*item) if isinstance(item[0], tuple) else pltpu.VMEM(item, F32)
             for item in scratch
         ]
-        sems = [(5,), (2,), (2,)] + [()] * 8 + [(2, ENDS), (2,), (2,), (2,)]
+        sems = [(6,), (2,), (2,)] + [()] * 8 + [(2, ENDS), (2,), (2,), (2,)]
         made = pl.pallas_call(
             functools.partial(kernel, n_lon, n_lat),
             out_shape=pltpu.VMEM((FIELDS, LEV * ROWS, LANES), F32),

time: 24.1 us -> 24.1 us (level)
  no operation moved by 1% of the time
where the time goes in v6:
time: 24.1 us; the launch traced here: 24 us
  Pallas kernels  23.3 us (97%)
  local copies, waits for them, and re-layouts  0.68 us (3%)
    pallas_call x1, Pallas kernels, per_device(): pl.pallas_call(functools.partial(kernel, n_lon, n_lat), out_shape=pltpu.V...  23.3 us
    unnamed x1, local copies, waits for them, and re-layouts  0.68 us

profile of v6, /device:TPU:1, one launch (start us, length us, event | category | flops | bytes accessed | tf_op | source)
XLA Modules:
  0.0 24.0 jit_solution(14453818240914110840)
XLA Ops:
  0.0 23.3 %shard_map.55 = f32[2,200,128]{2,1,0:T(8,128)S(1)} custom-call(f32[2,25,8,128]{3,2,1,0:T(8,128)} %tr_h.1, s32[25,8,128]{2,1,0:T(8,128)} %mk_h.1, bf16[25,8,128]{2,1,0:T(8,128)(2,1)} %kl_h.1, bf16[25,8,128]{2,1,0:T(8,128)(2,1)} %kt_h.1, f32[25,2,25]{2,1,0:T(2,128)} %bitcast.3), custom_call_target="tpu_custom_call" | custom-call | tf_op jit(solution)/shard_map/pallas_call | solution.py:583
  23.3 0.7 %copy.7 = f32[2,25,8,128]{3,2,1,0:T(8,128)} copy(f32[2,25,8,128]{3,2,1,0:T(8,128)S(1)} %bitcast.2) | data formatting | bytes 409600

commit v7 on v5

--- a/solution.py
+++ b/solution.py
@@ -256,21 +256,6 @@
             two_g[core, 0:HALF, 2 * q + h, :] = value[h, :HALF]
     to_mate(two_g, two_ss.at[0], two_rs.at[0]).start()
     for t in range(4):
-        tile = roll(lat_s[pl.ds(STARTS[t] * ROWS, ROWS), :], 8)
-        for g in range(1, COUNTS[t]):
-            tile = pick(
-                group == 8 - g, roll(lat_s[pl.ds((STARTS[t] + g) * ROWS, ROWS), :], 8 - 16 * g), tile
-            )
-        for f in range(FIELDS):
-            edge_c[pl.ds((4 * f + t) * ROWS, ROWS), :] = tile
-    coef = [by_row(edge_c, y) for y in range(ROWS)]
-    unused, unused, g1, g8 = factor(coef)
-    for y in range(ROWS):
-        edge_g1[y], edge_g8[y] = g1[y], g8[y]
-    for q, value in enumerate((g1[0], g8[-1], g8[0], coef[0], coef[-1])):
-        msg_ge[q] = value[0:4]
-
-    for t in range(4):
         n = COUNTS[t]
         coefs = lon_s[0, t, pl.ds(0, n)]
         face_east = jnp.minimum(coefs, roll(coefs, -1))
@@ -291,6 +276,7 @@
 
     to_mate(two_p, two_ss.at[1], two_rs.at[1]).start()
 
+
     def lower(q):
         return two_g[0, :, 2 * q : 2 * q + 2, :]
 
@@ -309,6 +295,22 @@
         for q, value in enumerate((weight, low_g, up_g)):
             joint_s[q, :, 2 * f : 2 * f + 2, :] = value
     send_to_hosts(msg_g, got_g, g_ss, g_rs)
+
+    for t in range(4):
+        tile = roll(lat_s[pl.ds(STARTS[t] * ROWS, ROWS), :], 8)
+        for g in range(1, COUNTS[t]):
+            tile = pick(
+                group == 8 - g, roll(lat_s[pl.ds((STARTS[t] + g) * ROWS, ROWS), :], 8 - 16 * g), tile
+            )
+        for f in range(FIELDS):
+            edge_c[pl.ds((4 * f + t) * ROWS, ROWS), :] = tile
+    coef = [by_row(edge_c, y) for y in range(ROWS)]
+    unused, unused, g1, g8 = factor(coef)
+    for y in range(ROWS):
+        edge_g1[y], edge_g8[y] = g1[y], g8[y]
+    for q, value in enumerate((g1[0], g8[-1], g8[0], coef[0], coef[-1])):
+        msg_ge[q] = value[0:4]
+
     to_mate(two_p, two_ss.at[1], two_rs.at[1]).wait_recv()
     jump = two_p[1, :, 0:4, :] - two_p[0, :, 4:8, :]
     msg_p[:, 0:4, :] = two_p[0, :, 0:4, :] + joint_s[1] * jump

time: 24.1 us -> 24.2 us (level)
  no operation moved by 1% of the time
where the time goes in v7:
time: 24.2 us; the launch traced here: 24 us
  Pallas kernels  23.4 us (97%)
  local copies, waits for them, and re-layouts  0.68 us (3%)
    pallas_call x1, Pallas kernels, per_device(): pl.pallas_call(functools.partial(kernel, n_lon, n_lat), out_shape=pltpu.V...  23.4 us
    unnamed x1, local copies, waits for them, and re-layouts  0.68 us

profile of v7, /device:TPU:1, one launch (start us, length us, event | category | flops | bytes accessed | tf_op | source)
XLA Modules:
  0.0 24.0 jit_solution(6789850941666812203)
XLA Ops:
  0.0 23.4 %shard_map.55 = f32[2,200,128]{2,1,0:T(8,128)S(1)} custom-call(f32[2,25,8,128]{3,2,1,0:T(8,128)} %tr_h.1, s32[25,8,128]{2,1,0:T(8,128)} %mk_h.1, bf16[25,8,128]{2,1,0:T(8,128)(2,1)} %kl_h.1, bf16[25,8,128]{2,1,0:T(8,128)(2,1)} %kt_h.1, f32[25,2,25]{2,1,0:T(2,128)} %bitcast.3), custom_call_target="tpu_custom_call" | custom-call | tf_op jit(solution)/shard_map/pallas_call | solution.py:581
  23.4 0.7 %copy.7 = f32[2,25,8,128]{3,2,1,0:T(8,128)} copy(f32[2,25,8,128]{3,2,1,0:T(8,128)S(1)} %bitcast.2) | data formatting | bytes 409600
